TPU v7x, 32 devices: a whole 2x2x4 slice. The times are simulated.
32 devices in a mesh: tgt: 4 (over y, x), hist: 8 (over z, core).
Axes of the slice: x: 2, y: 2, z: 4, core: 2. Of those that a mesh axis runs over, the one named last changes fastest.
Arguments:
- history: float32 [2, 32, 32, 128, 128], P(None, 'hist', 'tgt'), may hold values from -6 to 6
- self_energy: float32 [2, 32, 128, 128], P(None, 'hist'), may hold values from -6 to 6
- green_row: float32 [2, 32, 128, 128], P(None, 'tgt'), may hold values from -6 to 6
- propagator: float32 [2, 128, 128], replicated, may hold values from -0.375 to 0.375
Outputs:
- new_rows: float32 [4, 2, 32, 128, 128], P(None, None, 'tgt', 'hist')
All inputs are finite; a program needn't handle non-finite values.
Results may differ from a plain program's by a relative error of at most 0.00016.
Values sent between devices are 32-bit elements; how exact they have to be, the bound alone decides.
A program may use at most 64 MiB of HBM per device.

v0:
```python
import jax
import jax.numpy as jnp
from jax import lax
from jax.sharding import PartitionSpec as P

STEPS = 4


COUPLING = 1.5
MIXING = 0.7


def from_root(value, axis, source):
    kept = jnp.where(lax.axis_index(axis) == source, value, 0).astype(value.dtype)
    return lax.psum(kept, axis)


def complex_product(left, right, form):
    highest = lax.Precision.HIGHEST
    real_part = jnp.einsum(form, left[0], right[0], precision=highest) - jnp.einsum(
        form, left[1], right[1], precision=highest
    )
    imag_part = jnp.einsum(form, left[0], right[1], precision=highest) + jnp.einsum(
        form, left[1], right[0], precision=highest
    )
    return (real_part, imag_part)


def self_energy_of(green):
    modulus = green[0] * green[0] + green[1] * green[1]
    factor = -COUPLING * modulus / (1.0 + modulus)
    return jnp.stack([factor * green[0], factor * green[1]])


def per_device(history, self_energy, green_row, propagator):
    hist_count = lax.axis_size("hist")
    hist_per_tgt = hist_count // lax.axis_size("tgt")
    hist_index = lax.axis_index("hist")
    local_times = history.shape[1]
    orbitals = green_row.shape[2]
    band_rows = orbitals // hist_count
    norm_factor = float(local_times * hist_count * orbitals) ** (-0.5)
    new_rows = []
    for step_index in range(STEPS):
        final_step = step_index == STEPS - 1
        local_terms = (
            jnp.stack(complex_product(self_energy, history, "sik,stkj->tij")) * norm_factor
        )
        collision = lax.psum_scatter(local_terms, "hist", scatter_dimension=2, tiled=True)
        prop_band = lax.dynamic_slice_in_dim(propagator, hist_index * band_rows, band_rows, 1)
        prop_real, prop_imag = complex_product(prop_band, green_row, "ik,tkj->tij")
        green_band = jnp.stack(
            [MIXING * (prop_real + collision[1]), MIXING * (prop_imag - collision[0])]
        )
        if not final_step:
            green_full = lax.all_gather(green_band, "hist", axis=2, tiled=True)
        new_rows.append(green_band)
        if not final_step:
            green_row = green_full
            energy = self_energy_of(green_full)
            sub_block = lax.dynamic_slice_in_dim(
                energy, hist_index % hist_per_tgt * local_times, local_times, 1
            )
            self_energy = from_root(sub_block, "tgt", hist_index // hist_per_tgt)
            owner_slot = jnp.where(hist_index == step_index, green_full, history[:, 0])
            history = history.at[:, 0].set(owner_slot)
    return jnp.stack(new_rows)


def solution(mesh):
    in_specs = (
        P(None, "hist", "tgt", None, None),
        P(None, "hist", None, None),
        P(None, "tgt", None, None),
        P(),
    )
    out_specs = P(None, None, "tgt", "hist", None)
    return jax.shard_map(
        per_device, mesh=mesh, in_specs=in_specs, out_specs=out_specs, check_vma=False
    )
```

profile of v0, /device:TPU:0, one launch (start us, length us, event | category | flops | bytes accessed | tf_op | source)
XLA Modules:
  0.0 424.9 jit_solution(3687788560363151843)
XLA Ops:
  6.5 5.4 %copy.5 = f32[2,4,8,128,128]{3,4,1,2,0:T(8,128)} copy(f32[2,4,8,128,128]{4,3,2,1,0:T(8,128)} %param.10) | data formatting | bytes 8388608 | tf_op args[0]
  12.0 4.0 fusion.29
  16.0 3.9 fusion.28
  19.9 2.3 fusion.33
  22.2 2.3 fusion.35
  26.4 34.3 %reduce-scatter.5.cloned.1.call-done = f32[2,8,16,128]{3,2,1,0:T(8,128)} async-done(((f32[2,8,128,128]{3,2,1,0:T(8,128)}), f32[2,8,16,128]{3,2,1,0:T(8,128)}) %reduce-scatter.5.cloned.1.call-update) | async-done | bytes 131088 | tf_op jit(solution)/shard_map/reduce_scatter | solution.py:49
  63.9 20.6 %all-gather.4.cloned.1.call-done = f32[2,8,128,128]{3,2,1,0:T(8,128)} async-done(((f32[2,8,16,128]{3,2,1,0:T(8,128)}), f32[2,8,128,128]{3,2,1,0:T(8,128)}) %all-gather.4.cloned.1.call-update) | async-done | bytes 1048592 | tf_op jit(solution)/shard_map/all_gather | solution.py:56
  84.5 1.5 fusion.114
  89.8 42.7 %all-reduce.4.cloned.1.call-done = f32[2,4,128,128]{3,2,1,0:T(8,128)} async-done(((f32[2,4,128,128]{3,2,1,0:T(8,128)}), f32[2,4,128,128]{3,2,1,0:T(8,128)}) %all-reduce.4.cloned.1.call-update) | async-done | bytes 524304 | tf_op jit(solution)/shard_map/psum | solution.py:15
  132.5 4.0 fusion.25
  136.5 3.9 fusion.24
  140.4 2.3 fusion.37
  142.7 2.3 fusion.39
  147.0 31.6 %reduce-scatter.7.cloned.1.call-done = f32[2,8,16,128]{3,2,1,0:T(8,128)} async-done(((f32[2,8,128,128]{3,2,1,0:T(8,128)}), f32[2,8,16,128]{3,2,1,0:T(8,128)}) %reduce-scatter.7.cloned.1.call-update) | async-done | bytes 131088 | tf_op jit(solution)/shard_map/reduce_scatter | solution.py:49
  181.8 20.5 %all-gather.6.cloned.1.call-done = f32[2,8,128,128]{3,2,1,0:T(8,128)} async-done(((f32[2,8,16,128]{3,2,1,0:T(8,128)}), f32[2,8,128,128]{3,2,1,0:T(8,128)}) %all-gather.6.cloned.1.call-update) | async-done | bytes 1048592 | tf_op jit(solution)/shard_map/all_gather | solution.py:56
  202.3 1.5 fusion.112
  206.0 1.6 copy.18
  208.6 41.5 %all-reduce.6.cloned.1.call-done = f32[2,4,128,128]{3,2,1,0:T(8,128)} async-done(((f32[2,4,128,128]{3,2,1,0:T(8,128)}), f32[2,4,128,128]{3,2,1,0:T(8,128)}) %all-reduce.6.cloned.1.call-update) | async-done | bytes 524304 | tf_op jit(solution)/shard_map/psum | solution.py:15
  250.2 4.0 fusion.21
  254.2 3.9 fusion.20
  258.1 2.3 fusion.41
  260.4 2.3 fusion.43
  264.7 31.6 %reduce-scatter.9.cloned.1.call-done = f32[2,8,16,128]{3,2,1,0:T(8,128)} async-done(((f32[2,8,128,128]{3,2,1,0:T(8,128)}), f32[2,8,16,128]{3,2,1,0:T(8,128)}) %reduce-scatter.9.cloned.1.call-update) | async-done | bytes 131088 | tf_op jit(solution)/shard_map/reduce_scatter | solution.py:49
  299.5 20.6 %all-gather.8.cloned.1.call-done = f32[2,8,128,128]{3,2,1,0:T(8,128)} async-done(((f32[2,8,16,128]{3,2,1,0:T(8,128)}), f32[2,8,128,128]{3,2,1,0:T(8,128)}) %all-gather.8.cloned.1.call-update) | async-done | bytes 1048592 | tf_op jit(solution)/shard_map/all_gather | solution.py:56
  320.1 1.5 fusion.110
  323.9 1.6 copy.23
  326.5 41.6 %all-reduce.8.cloned.1.call-done = f32[2,4,128,128]{3,2,1,0:T(8,128)} async-done(((f32[2,4,128,128]{3,2,1,0:T(8,128)}), f32[2,4,128,128]{3,2,1,0:T(8,128)}) %all-reduce.8.cloned.1.call-update) | async-done | bytes 524304 | tf_op jit(solution)/shard_map/psum | solution.py:15
  368.1 4.0 fusion.17
  372.1 3.9 fusion.16
  376.0 2.3 fusion.45
  378.3 2.3 fusion.47
  382.5 31.7 %reduce-scatter.11.cloned.1.call-done = f32[2,8,16,128]{3,2,1,0:T(8,128)} async-done(((f32[2,8,128,128]{3,2,1,0:T(8,128)}), f32[2,8,16,128]{3,2,1,0:T(8,128)}) %reduce-scatter.11.cloned.1.call-update) | async-done | bytes 131088 | tf_op jit(solution)/shard_map/reduce_scatter | solution.py:49
  (83 shorter events, 31.1 us)
Async XLA Ops:
  6.5 19.1 %copy-start = (f32[2,128,128]{2,1,0:T(8,128)S(1)}, f32[2,128,128]{2,1,0:T(8,128)}, u32[]{:S(2)}) copy-start(f32[2,128,128]{2,1,0:T(8,128)} %param.13) | copy-start | bytes 393220
  6.5 5.4 %copy-start.9 = (f32[2,4,128,128]{3,2,1,0:T(8,128)S(1)}, f32[2,4,128,128]{3,2,1,0:T(8,128)}, u32[]{:S(2)}) copy-start(f32[2,4,128,128]{3,2,1,0:T(8,128)} %param.11) | copy-start | bytes 1572868
  6.5 54.1 %reduce-scatter.5.cloned.1.call-start = ((), (), s32[]{:S(2)}) async-start(), calls=%async_computation.4 | async-start | bytes 1179648 | tf_op jit(solution)/shard_map/reduce_scatter | solution.py:49
  12.0 7.9 %copy-start.1 = (f32[2,4,8,128,128]{3,4,1,2,0:T(8,128)S(1)}, f32[2,4,8,128,128]{3,4,1,2,0:T(8,128)}, u32[]{:S(2)}) copy-start(f32[2,4,8,128,128]{3,4,1,2,0:T(8,128)} %copy.5) | copy-start | bytes 12582916
  19.8 5.8 %copy-start.8 = (f32[2,8,128,128]{3,2,1,0:T(8,128)S(1)}, f32[2,8,128,128]{3,2,1,0:T(8,128)}, u32[]{:S(2)}) copy-start(f32[2,8,128,128]{3,2,1,0:T(8,128)} %param.12) | copy-start | bytes 3145732
  25.6 58.9 %all-gather.4.cloned.1.call-start = ((), (), s32[]{:S(2)}) async-start(), calls=%async_computation.5 | async-start | bytes 1179648 | tf_op jit(solution)/shard_map/all_gather | solution.py:56
  63.8 68.7 %all-reduce.4.cloned.1.call-start = ((), (), s32[]{:S(2)}) async-start(), calls=%async_computation.6 | async-start | bytes 1048576 | tf_op jit(solution)/shard_map/psum | solution.py:15
  84.5 2.6 copy-start.6
  86.8 91.8 %reduce-scatter.7.cloned.1.call-start = ((), (), s32[]{:S(2)}) async-start(), calls=%async_computation.7 | async-start | bytes 1179648 | tf_op jit(solution)/shard_map/reduce_scatter | solution.py:49
  132.5 7.9 %copy-start.2 = (f32[2,4,8,128,128]{3,4,1,2,0:T(8,128)S(1)}, f32[2,4,8,128,128]{3,4,1,2,0:T(8,128)}, u32[]{:S(2)}) copy-start(f32[2,4,8,128,128]{3,4,1,2,0:T(8,128)} %constant_dynamic-update-slice_fusion.2) | copy-start | bytes 12582916
  132.5 7.9 %copy-start.11 = (f32[2,4,128,128]{3,2,1,0:T(8,128)S(1)}, f32[2,4,128,128]{3,2,1,0:T(8,128)}, u32[]{:S(2)}) copy-start(f32[2,4,128,128]{3,2,1,0:T(8,128)} %all-reduce.4.cloned.1.call-done) | copy-start | bytes 1572868
  146.1 56.2 %all-gather.6.cloned.1.call-start = ((), (), s32[]{:S(2)}) async-start(), calls=%async_computation.8 | async-start | bytes 1179648 | tf_op jit(solution)/shard_map/all_gather | solution.py:56
  181.8 68.4 %all-reduce.6.cloned.1.call-start = ((), (), s32[]{:S(2)}) async-start(), calls=%async_computation.9 | async-start | bytes 1048576 | tf_op jit(solution)/shard_map/psum | solution.py:15
  202.3 2.6 copy-start.5
  204.6 91.6 %reduce-scatter.9.cloned.1.call-start = ((), (), s32[]{:S(2)}) async-start(), calls=%async_computation.10 | async-start | bytes 1179648 | tf_op jit(solution)/shard_map/reduce_scatter | solution.py:49
  250.2 7.9 %copy-start.3 = (f32[2,4,8,128,128]{3,4,1,2,0:T(8,128)S(1)}, f32[2,4,8,128,128]{3,4,1,2,0:T(8,128)}, u32[]{:S(2)}) copy-start(f32[2,4,8,128,128]{3,4,1,2,0:T(8,128)} %constant_dynamic-update-slice_fusion.1) | copy-start | bytes 12582916
  250.2 7.9 %copy-start.12 = (f32[2,4,128,128]{3,2,1,0:T(8,128)S(1)}, f32[2,4,128,128]{3,2,1,0:T(8,128)}, u32[]{:S(2)}) copy-start(f32[2,4,128,128]{3,2,1,0:T(8,128)} %all-reduce.6.cloned.1.call-done) | copy-start | bytes 1572868
  263.8 56.3 %all-gather.8.cloned.1.call-start = ((), (), s32[]{:S(2)}) async-start(), calls=%async_computation.11 | async-start | bytes 1179648 | tf_op jit(solution)/shard_map/all_gather | solution.py:56
  299.5 68.6 %all-reduce.8.cloned.1.call-start = ((), (), s32[]{:S(2)}) async-start(), calls=%async_computation.12 | async-start | bytes 1048576 | tf_op jit(solution)/shard_map/psum | solution.py:15
  320.1 2.6 copy-start.7
  322.4 91.8 %reduce-scatter.11.cloned.1.call-start = ((), (), s32[]{:S(2)}) async-start(), calls=%async_computation.13 | async-start | bytes 1179648 | tf_op jit(solution)/shard_map/reduce_scatter | solution.py:49
  368.1 7.9 %copy-start.4 = (f32[2,4,8,128,128]{3,4,1,2,0:T(8,128)S(1)}, f32[2,4,8,128,128]{3,4,1,2,0:T(8,128)}, u32[]{:S(2)}) copy-start(f32[2,4,8,128,128]{3,4,1,2,0:T(8,128)} %constant_dynamic-update-slice_fusion) | copy-start | bytes 12582916
  368.1 7.9 %copy-start.10 = (f32[2,4,128,128]{3,2,1,0:T(8,128)S(1)}, f32[2,4,128,128]{3,2,1,0:T(8,128)}, u32[]{:S(2)}) copy-start(f32[2,4,128,128]{3,2,1,0:T(8,128)} %all-reduce.8.cloned.1.call-done) | copy-start | bytes 1572868
  378.3 38.4 %copy-start.13 = (f32[1,2,8,16,128]{4,3,2,1,0:T(8,128)S(1)}, f32[1,2,8,16,128]{4,3,2,1,0:T(8,128)}, u32[]{:S(2)}) copy-start(f32[1,2,8,16,128]{4,3,2,1,0:T(8,128)} %get-tuple-element.51) | copy-start | bytes 393220
Sparse Core Ops, SparseCore 0:
  25.7 34.9 reduce-scatter.4
  63.9 20.5 all-gather.3
  87.5 44.9 all-reduce.3
  146.3 32.3 reduce-scatter.6
  181.9 20.3 all-gather.5
  205.2 44.9 all-reduce.5
  263.9 32.2 reduce-scatter.8
  299.6 20.4 all-gather.7
  323.1 44.9 all-reduce.7
  381.9 32.3 reduce-scatter.10
where the time goes:
time: 432 us; the launch traced here: 425 us
  waiting for transfers between devices  317 us (73%)
  matrix products  62.9 us (15%)
  other arithmetic  17.8 us (4%)
  between operations  14.3 us (3%)
  local copies, waits for them, and re-layouts  12 us (3%)
    reduce_scatter x4, waiting for transfers between devices, per_device(): lax.psum_scatter(local_terms, 'hist', scatter_dimension=2, tiled=True)  129 us
    psum x3, waiting for transfers between devices, from_root(): return lax.psum(kept, axis)  126 us
    all_gather x3, waiting for transfers between devices, per_device(): green_full = lax.all_gather(green_band, 'hist', axis=2, tiled=True)  61.7 us
    dot_general x8, matrix products, complex_product(): jnp.einsum(form, left[1], right[1], precision=highest)  20.4 us
    dot_general x8, matrix products, complex_product(): jnp.einsum(form, left[0], right[1], precision=highest)  17.6 us
    dot_general x8, matrix products, complex_product(): jnp.einsum(form, left[1], right[0], precision=highest)  14.1 us
    dot_general x8, matrix products, complex_product(): jnp.einsum(form, left[0], right[0], precision=highest)  10.8 us
  transfers between devices with their start and end apart: 10, of which 10 were waited for; matrix products, arithmetic and copies ran while one was open for 3% of the time, Pallas kernels for 0%

commit v1 on v0

v1 whole, which is shorter than its diff:
```python
import functools

import jax
import jax.numpy as jnp
from jax import lax
from jax.experimental import pallas as pl
from jax.experimental.pallas import tpu as pltpu
from jax.sharding import PartitionSpec as P

STEPS = 4
COUPLING = 1.5
MIXING = 0.7
MESH = pl.DeviceIdType.MESH
F32, BF16 = jnp.float32, jnp.bfloat16


def split(value):
    high = value.astype(BF16)
    return high, (value - high.astype(F32)).astype(BF16)


def complex_of(product):
    n = product.shape[0] // 2
    return product[:n, :n] - product[n:, n:], product[:n, n:] + product[n:, :n]


def snake(index):
    q, r = index // 2, index % 2
    return 2 * q + r + (q % 2) * (1 - 2 * r)


def kernel(
    n_tgt, n_hist, norm,
    h_hbm, s_hbm, r_hbm, p_hbm, out_ref,
    hst, h3, s3, sbuf, rin, pin, exs, exr, own, upb, dnb, rows, x3, base, sxb, l3, outb,
    fin, exf, fsum, upf, dnf,
    h_sem, in_sem, ex_s, ex_r, ch_s, up_r, dn_r, rg_s, rg_r, sx_s, sx_r, bd_s, bd_r,
    fx_s, fx_r, fc_s, fu_r, fd_r,
):
    _, sh, tt_all, n, _ = h_hbm.shape
    hp = n_hist // n_tgt
    nz = n_hist // hp
    band = n // n_hist
    depth = sh * n
    g, h = lax.axis_index("tgt"), lax.axis_index("hist")
    z, c = h // hp, h % hp
    root = z == g
    pos = snake(g)
    rel = (pos - snake(z) + n_tgt) % n_tgt
    ahead, behind = snake((pos + 1) % n_tgt), snake((pos + n_tgt - 1) % n_tgt)
    last = STEPS - 1
    sends = []

    def remote(src, dst, send_sem, recv_sem, tgt, hist):
        return pltpu.make_async_remote_copy(
            src_ref=src, dst_ref=dst, send_sem=send_sem, recv_sem=recv_sem,
            device_id={"tgt": tgt, "hist": hist}, device_id_type=MESH,
        )

    def loop(count, body):
        lax.fori_loop(0, count, lambda i, _: (body(i), None)[1], None)

    def h_copy(t):
        return pltpu.make_async_copy(h_hbm.at[:, :, t], hst.at[t], h_sem.at[t])

    s_copy = pltpu.make_async_copy(s_hbm, sbuf.at[0], in_sem.at[0])
    p_copy = pltpu.make_async_copy(p_hbm, pin, in_sem.at[1])
    r_copy = pltpu.make_async_copy(r_hbm, rin, in_sem.at[2])
    s_copy.start()
    for d in [*range(1, hp), 0]:
        loop(sh, lambda t, d=d: h_copy((c + d) % hp * sh + t).start())
    p_copy.start()
    r_copy.start()

    barrier = pltpu.get_barrier_semaphore()
    for e in range(1, n_hist):
        pl.semaphore_signal(
            barrier, inc=1, device_id={"tgt": g, "hist": (h + e) % n_hist}, device_id_type=MESH
        )
    for near in (ahead, behind):
        pl.semaphore_signal(barrier, inc=1, device_id={"tgt": near, "hist": h}, device_id_type=MESH)

    def store_x3(slot, tt, real, imag):
        for at, value in ((0, real), (n, imag)):
            high, low = split(value)
            cols = pl.ds(at, n)
            x3[slot, tt, pl.ds(0, n), cols] = high
            x3[slot, tt, pl.ds(n, n), cols] = low
            x3[slot, tt, pl.ds(2 * n, n), cols] = high

    def store_l3(slot, real, imag):
        for at, value in ((0, real), (n, imag)):
            high, low = split(value)
            l3[slot, pl.ds(at, n), pl.ds(0, n)] = high
            l3[slot, pl.ds(at, n), pl.ds(n, n)] = high
            l3[slot, pl.ds(at, n), pl.ds(2 * n, n)] = low

    def store_s3(step):
        for s in range(sh):
            for part in range(2):
                high, low = split(sbuf[step, part, s])
                r = pl.ds(part * n, n)
                s3[r, pl.ds(s * n, n)] = high
                s3[r, pl.ds(depth + s * n, n)] = high
                s3[r, pl.ds(2 * depth + s * n, n)] = low
        if step > 0:

            @pl.when(h < step)
            def _():
                for at in range(3):
                    s3[:, pl.ds(at * depth, n)] = jnp.zeros((2 * n, n), BF16)

    def store_h3(t):
        h_copy(t).wait()
        for s in range(sh):
            for part in range(2):
                high, low = split(hst[t, part, s])
                cols = pl.ds(part * n, n)
                h3[t, pl.ds(s * n, n), cols] = high
                h3[t, pl.ds(depth + s * n, n), cols] = low
                h3[t, pl.ds(2 * depth + s * n, n), cols] = high

    def term(t, step):
        if step == 0:
            store_h3(t)
        real, imag = complex_of(jnp.dot(s3[...], h3[t], preferred_element_type=F32))
        return (MIXING * norm) * imag, (-MIXING * norm) * real

    def ex_copy(step, d, tt):
        return remote(
            exs.at[step, d, tt], exr.at[step, d, tt], ex_s.at[step, d, tt], ex_r.at[step, d, tt],
            g, z * hp + (c + d) % hp,
        )

    def chain_copy(step, tt, up):
        return remote(
            own.at[step, tt], (upb if up else dnb).at[step, tt], ch_s.at[step, tt],
            (up_r if up else dn_r).at[step, tt], g, h + hp if up else h - hp,
        )

    def ring_copy(step, part, s):
        ref = sbuf.at[step, part, s]
        return remote(
            ref, ref, rg_s.at[step, part, s], rg_r.at[step, part, s],
            behind if part else ahead, h,
        )

    ring_gets = (rel > 0, rel > 0)
    ring_gives = (rel < n_tgt - 1, rel != 1)

    def sx_copy(step, k, to):
        return remote(
            sbuf.at[step, :, 0], sxb.at[step, k], sx_s.at[step, k, to], sx_r.at[step, k],
            g, g * hp + to,
        )

    def band_copy(step, e, sender):
        to = (h + e) % n_hist
        return remote(
            rows.at[step, :, :, pl.ds(pl.multiple_of(to * band, band), band)],
            outb.at[step, :, pl.ds(sender * sh, sh)], bd_s.at[step, e], bd_r.at[step, sender],
            g, to,
        )

    def fin_ex_copy(q, d):
        to = (c + d) % hp
        return remote(
            fin.at[q, :, to], exf.at[q, d], fx_s.at[q, d], fx_r.at[q, d], g, z * hp + to
        )

    def fin_chain_copy(q, zz, up):
        return remote(
            fsum.at[q, zz], (upf if up else dnf).at[q, zz], fc_s.at[q, zz],
            (fu_r if up else fd_r).at[q, zz], g, h + hp if up else h - hp,
        )

    def receive_s(step):
        def one(s):
            for part in range(2):

                @pl.when(ring_gets[part])
                def _():
                    ring_copy(step, part, s).wait_recv()

                    @pl.when(ring_gives[part])
                    def _():
                        ring_copy(step, part, s).start()

        loop(sh, one)
        for part in range(2):
            sends.append(
                (ring_gives[part], lambda part=part: loop(sh, lambda s: ring_copy(step, part, s).wait_send()))
            )
        for k in range(min(step, n_hist)):
            for to in range(hp):
                mine = g * hp + to == h

                @pl.when((h == k) & mine)
                def _():
                    sxb[step, k] = sbuf[step, :, 0]

                away = (h == k) & (g * hp + to != h)

                @pl.when(away)
                def _():
                    sx_copy(step, k, to).start()

                sends.append((away, lambda k=k, to=to: sx_copy(step, k, to).wait_send()))

    def make_base(step):
        for k in range(min(step, n_hist)):

            @pl.when(h != k)
            def _():
                sx_copy(step, k, 0).wait_recv()

            store_l3(k + 1, norm * sxb[step, k, 1], -norm * sxb[step, k, 0])

        def one(tt):
            total = jnp.dot(l3[0], x3[step, tt], preferred_element_type=F32)
            for k in range(min(step, n_hist)):
                total += jnp.dot(l3[k + 1], x3[k + 1, tt], preferred_element_type=F32)
            real, imag = complex_of(total)
            base[tt, 0] = MIXING * real
            base[tt, 1] = MIXING * imag

        loop(sh, one)

    s_copy.wait()
    store_s3(0)
    pl.semaphore_wait(barrier, n_hist + 1)

    for step in range(last):
        if step > 0:
            receive_s(step)
            store_s3(step)

        for d in range(1, hp):

            def give(tt, d=d):
                real, imag = term((c + d) % hp * sh + tt, step)
                exs[step, d, tt, 0] = real
                exs[step, d, tt, 1] = imag
                ex_copy(step, d, tt).start()

            loop(sh, give)
            sends.append((None, lambda d=d, step=step: loop(sh, lambda tt: ex_copy(step, d, tt).wait_send())))

        def keep(tt):
            real, imag = term(c * sh + tt, step)
            own[step, tt, 0] = real
            own[step, tt, 1] = imag
            for d in range(1, hp):
                ex_copy(step, d, tt).wait_recv()
                own[step, tt] += exr[step, d, tt]

            @pl.when((z < g) & (z == 0))
            def _():
                chain_copy(step, tt, True).start()

            @pl.when((z > g) & (z == nz - 1))
            def _():
                chain_copy(step, tt, False).start()

        loop(sh, keep)
        if step == 0:
            p_copy.wait()
            r_copy.wait()

        @pl.when(root)
        def _():
            if step == 0:
                store_l3(0, pin[0], pin[1])
                loop(sh, lambda tt: store_x3(0, tt, rin[0, c * sh + tt], rin[1, c * sh + tt]))
            make_base(step)

        def link(tt):
            @pl.when((z > 0) & (z <= g))
            def _():
                chain_copy(step, tt, True).wait_recv()
                own[step, tt] += upb[step, tt]

            @pl.when((z < nz - 1) & (z >= g))
            def _():
                chain_copy(step, tt, False).wait_recv()
                own[step, tt] += dnb[step, tt]

            @pl.when((z < g) & (z > 0))
            def _():
                chain_copy(step, tt, True).start()

            @pl.when((z > g) & (z < nz - 1))
            def _():
                chain_copy(step, tt, False).start()

            @pl.when(root)
            def _():
                real = own[step, tt, 0] + base[tt, 0]
                imag = own[step, tt, 1] + base[tt, 1]
                modulus = real * real + imag * imag
                factor = -COUPLING * modulus / (1.0 + modulus)
                sbuf[step + 1, 0, tt] = factor * real
                sbuf[step + 1, 1, tt] = factor * imag
                ring_copy(step + 1, 0, tt).start()
                ring_copy(step + 1, 1, tt).start()
                rows[step, 0, tt] = real
                rows[step, 1, tt] = imag
                store_x3(step + 1, tt, real, imag)

        loop(sh, link)
        for up, gives in ((True, z < g), (False, z > g)):
            sends.append(
                (gives, lambda up=up, step=step: loop(sh, lambda tt: chain_copy(step, tt, up).wait_send()))
            )

        @pl.when(root)
        def _():
            outb[step, :, pl.ds(c * sh, sh)] = rows[
                step, :, :, pl.ds(pl.multiple_of(h * band, band), band)
            ]
            loop(n_hist - 1, lambda e: band_copy(step, e + 1, c).start())

        sends.append(
            (root, lambda step=step: loop(n_hist - 1, lambda e: band_copy(step, e + 1, c).wait_send()))
        )

    receive_s(last)
    store_s3(last)
    pl.when(root)(lambda: make_base(last))
    for q in range(hp):

        def bands(tt, q=q):
            for part, value in enumerate(term(q * sh + tt, last)):
                for b in range(n_hist):
                    fin[q, b // hp, b % hp, tt, part] = value[b * band : (b + 1) * band]

        loop(sh, bands)

        @pl.when(root & (c == q))
        def _():
            def add(tt):
                for part in range(2):
                    for b in range(n_hist):
                        fin[q, b // hp, b % hp, tt, part] += base[tt, part, pl.ds(b * band, band)]

            loop(sh, add)

        for d in range(1, hp):
            fin_ex_copy(q, d).start()
            sends.append((None, lambda q=q, d=d: fin_ex_copy(q, d).wait_send()))

    for q in range(hp):
        for d in range(1, hp):
            fin_ex_copy(q, d).wait_recv()

        def both(zz, q=q):
            value = fin[q, zz, c]
            for d in range(1, hp):
                value += exf[q, d, zz]
            fsum[q, zz] = value

        loop(nz, both)
        for dist in range(nz - 1, 0, -1):
            for up in (True, False):
                zz = z + dist if up else z - dist
                on_way = zz < nz if up else zz >= 0
                first = z == 0 if up else z == nz - 1

                @pl.when(on_way)
                def _():
                    @pl.when(jnp.logical_not(first))
                    def _():
                        fin_chain_copy(q, zz, up).wait_recv()
                        fsum[q, zz] += (upf if up else dnf)[q, zz]

                    fin_chain_copy(q, zz, up).start()

                sends.append(
                    (on_way, lambda q=q, zz=zz, up=up: fin_chain_copy(q, zz, up).wait_send())
                )
    for q in range(hp):

        @pl.when(z > 0)
        def _():
            fin_chain_copy(q, z, True).wait_recv()
            fsum[q, z] += upf[q, z]

        @pl.when(z < nz - 1)
        def _():
            fin_chain_copy(q, z, False).wait_recv()
            fsum[q, z] += dnf[q, z]

        for tt in range(sh):
            for part in range(2):
                out_ref[last, part, q * sh + tt] = fsum[q, z, tt, part]

    for step in range(last):
        for sender in range(hp):

            @pl.when(h != g * hp + sender)
            def _():
                band_copy(step, 1, sender).wait_recv()

        out_ref[step] = outb[step]

    for gives, wait in sends:
        if gives is None:
            wait()
        else:
            pl.when(gives)(wait)


def per_device(history, self_energy, green_row, propagator):
    n_tgt, n_hist = lax.axis_size("tgt"), lax.axis_size("hist")
    _, sh, tt, n, _ = history.shape
    hp, band, last = n_hist // n_tgt, n // n_hist, STEPS - 1
    nz = n_hist // hp
    norm = float(sh * n_hist * n) ** (-0.5)
    vmem, sem = pltpu.VMEM, pltpu.SemaphoreType.DMA
    return pl.pallas_call(
        functools.partial(kernel, n_tgt, n_hist, norm),
        out_shape=jax.ShapeDtypeStruct((STEPS, 2, tt, band, n), F32),
        in_specs=[pl.BlockSpec(memory_space=pl.ANY)] * 4,
        out_specs=pl.BlockSpec(memory_space=pltpu.VMEM),
        scratch_shapes=[
            vmem((tt, 2, sh, n, n), F32),
            vmem((tt, 3 * sh * n, 2 * n), BF16),
            vmem((2 * n, 3 * sh * n), BF16),
            vmem((STEPS, 2, sh, n, n), F32),
            vmem((2, tt, n, n), F32),
            vmem((2, n, n), F32),
            vmem((last, hp, sh, 2, n, n), F32),
            vmem((last, hp, sh, 2, n, n), F32),
            vmem((last, sh, 2, n, n), F32),
            vmem((last, sh, 2, n, n), F32),
            vmem((last, sh, 2, n, n), F32),
            vmem((last, 2, sh, n, n), F32),
            vmem((STEPS, sh, 3 * n, 2 * n), BF16),
            vmem((sh, 2, n, n), F32),
            vmem((STEPS, STEPS, 2, n, n), F32),
            vmem((STEPS, 2 * n, 3 * n), BF16),
            vmem((last, 2, tt, band, n), F32),
            vmem((hp, nz, hp, sh, 2, band, n), F32),
            vmem((hp, hp, nz, sh, 2, band, n), F32),
            vmem((hp, nz, sh, 2, band, n), F32),
            vmem((hp, nz, sh, 2, band, n), F32),
            vmem((hp, nz, sh, 2, band, n), F32),
            sem((tt,)),
            sem((3,)),
            sem((last, hp, sh)),
            sem((last, hp, sh)),
            sem((last, sh)),
            sem((last, sh)),
            sem((last, sh)),
            sem((STEPS, 2, sh)),
            sem((STEPS, 2, sh)),
            sem((STEPS, STEPS, hp)),
            sem((STEPS, STEPS)),
            sem((last, n_hist)),
            sem((last, hp)),
            sem((hp, hp)),
            sem((hp, hp)),
            sem((hp, nz)),
            sem((hp, nz)),
            sem((hp, nz)),
        ],
        compiler_params=pltpu.CompilerParams(
            collective_id=0, has_side_effects=True, vmem_limit_bytes=56 * 2**20
        ),
    )(history, self_energy, green_row, propagator)


def solution(mesh):
    in_specs = (
        P(None, "hist", "tgt", None, None),
        P(None, "hist", None, None),
        P(None, "tgt", None, None),
        P(),
    )
    out_specs = P(None, None, "tgt", "hist", None)
    return jax.shard_map(
        per_device, mesh=mesh, in_specs=in_specs, out_specs=out_specs, check_vma=False
    )
```

time: 432 us -> 246 us (0.57)
  waiting for transfers between devices: 317 us -> 0 us
  Pallas kernels: 0 us -> 239 us
  matrix products: 62.9 us -> 0 us
  other arithmetic: 17.8 us -> 0 us
  between operations: 14.3 us -> 0.01 us
  local copies, waits for them, and re-layouts: 12 us -> 1.87 us
    pallas_call x0 -> x1, Pallas kernels: none -> 239 us  [per_device(): pl.pallas_call(functools.partial(kernel, n_tgt, n_hist, norm), out_shape=...]
    reduce_scatter x4 -> x0, waiting for transfers between devices: 129 us -> none  [per_device(): lax.psum_scatter(local_terms, 'hist', scatter_dimension=2, tiled=True)]
    psum x3 -> x0, waiting for transfers between devices: 126 us -> none  [from_root(): return lax.psum(kept, axis)]
    dot_general x32 -> x0, matrix products: 62.9 us -> none  [the longest x8 20.4 us: complex_product(): jnp.einsum(form, left[1], right[1], precision=highest)]
    all_gather x3 -> x0, waiting for transfers between devices: 61.7 us -> none  [per_device(): green_full = lax.all_gather(green_band, 'hist', axis=2, tiled=True)]
    mul x7 -> x0, other arithmetic: 8.7 us -> none  [the longest x3 4.36 us: self_energy_of(): return jnp.stack([factor * green[0], factor * green[1]])]
  transfers between devices with their start and end apart: 10 -> 0, of which waited for: 10 -> 0; matrix products, arithmetic and copies ran while one was open for 3% -> 0% of each run, Pallas kernels for 0% -> 0%
where the time goes in v1:
time: 246 us; the launch traced here: 241 us
  Pallas kernels  239 us (97%)
    pallas_call x1, Pallas kernels, per_device(): pl.pallas_call(functools.partial(kernel, n_tgt, n_hist, norm), out_shape=...  239 us

profile of v1, /device:TPU:0, one launch (start us, length us, event | category | flops | bytes accessed | tf_op | source)
XLA Modules:
  0.0 240.8 jit_solution(15075690545959964796)
XLA Ops:
  0.0 238.9 %shard_map.46 = f32[4,2,8,16,128]{4,3,2,1,0:T(8,128)} custom-call(f32[2,4,8,128,128]{4,3,2,1,0:T(8,128)} %h_hbm.1, f32[2,4,128,128]{3,2,1,0:T(8,128)} %s_hbm.1, f32[2,8,128,128]{3,2,1,0:T(8,128)} %r_hbm.1, f32[2,128,128]{2,1,0:T(8,128)} %p_hbm.1), custom_call_target="tpu_custom_call" | custom-call | tf_op jit(solution)/shard_map/pallas_call | solution.py:420
  238.9 1.9 copy.6

commit v2 on v1

--- a/solution.py
+++ b/solution.py
@@ -11,6 +11,7 @@
 COUPLING = 1.5
 MIXING = 0.7
 MESH = pl.DeviceIdType.MESH
+PIECES = 2
 F32, BF16 = jnp.float32, jnp.bfloat16
 
 
@@ -32,9 +33,9 @@
 def kernel(
     n_tgt, n_hist, norm,
     h_hbm, s_hbm, r_hbm, p_hbm, out_ref,
-    hst, h3, s3, sbuf, rin, pin, exs, exr, own, upb, dnb, rows, x3, base, sxb, l3, outb,
+    hst, h3, s3, acc, sbuf, rin, pin, exs, exr, own, upb, dnb, rows, x3, base, sxb, l3, outb,
     fin, exf, fsum, upf, dnf,
-    h_sem, in_sem, ex_s, ex_r, ch_s, up_r, dn_r, rg_s, rg_r, sx_s, sx_r, bd_s, bd_r,
+    h_sem, in_sem, ex_s, ex_r, ch_s, up_r, dn_r, rg_s, rg_r, sx_s, sy_s, sx_r, bd_s, bd_r,
     fx_s, fx_r, fc_s, fu_r, fd_r,
 ):
     _, sh, tt_all, n, _ = h_hbm.shape
@@ -95,20 +96,20 @@
             l3[slot, pl.ds(at, n), pl.ds(n, n)] = high
             l3[slot, pl.ds(at, n), pl.ds(2 * n, n)] = low
 
-    def store_s3(step):
-        for s in range(sh):
-            for part in range(2):
-                high, low = split(sbuf[step, part, s])
-                r = pl.ds(part * n, n)
-                s3[r, pl.ds(s * n, n)] = high
-                s3[r, pl.ds(depth + s * n, n)] = high
-                s3[r, pl.ds(2 * depth + s * n, n)] = low
-        if step > 0:
+    width = 3 * n
+
+    def store_s3(step, s):
+        for part in range(2):
+            high, low = split(sbuf[step, part, s])
+            r = pl.ds(part * n, n)
+            s3[r, pl.ds(s * width, n)] = high
+            s3[r, pl.ds(s * width + n, n)] = high
+            s3[r, pl.ds(s * width + 2 * n, n)] = low
+        if step > 0 and s == 0:
 
             @pl.when(h < step)
             def _():
-                for at in range(3):
-                    s3[:, pl.ds(at * depth, n)] = jnp.zeros((2 * n, n), BF16)
+                s3[:, pl.ds(0, width)] = jnp.zeros((2 * n, width), BF16)
 
     def store_h3(t):
         h_copy(t).wait()
@@ -116,14 +117,21 @@
             for part in range(2):
                 high, low = split(hst[t, part, s])
                 cols = pl.ds(part * n, n)
-                h3[t, pl.ds(s * n, n), cols] = high
-                h3[t, pl.ds(depth + s * n, n), cols] = low
-                h3[t, pl.ds(2 * depth + s * n, n), cols] = high
+                h3[t, pl.ds(s * width, n), cols] = high
+                h3[t, pl.ds(s * width + n, n), cols] = low
+                h3[t, pl.ds(s * width + 2 * n, n), cols] = high
+
+    def dot_of(t, begin, end):
+        at = pl.ds(begin * width, (end - begin) * width)
+        return jnp.dot(s3[:, at], h3[t, at, :], preferred_element_type=F32)
 
     def term(t, step):
         if step == 0:
             store_h3(t)
-        real, imag = complex_of(jnp.dot(s3[...], h3[t], preferred_element_type=F32))
+            product = dot_of(t, 0, sh)
+        else:
+            product = acc[t] + dot_of(t, sh - 1, sh)
+        real, imag = complex_of(product)
         return (MIXING * norm) * imag, (-MIXING * norm) * real
 
     def ex_copy(step, d, tt):
@@ -132,26 +140,43 @@
             g, z * hp + (c + d) % hp,
         )
 
-    def chain_copy(step, tt, up):
-        return remote(
-            own.at[step, tt], (upb if up else dnb).at[step, tt], ch_s.at[step, tt],
-            (up_r if up else dn_r).at[step, tt], g, h + hp if up else h - hp,
-        )
-
-    def ring_copy(step, part, s):
+    def piece(p):
+        per_part = PIECES // 2
+        return p // per_part, pl.ds(p % per_part * (n // per_part), n // per_part)
+
+    def chain_copy(step, tt, p, up):
+        part, at = piece(p)
+        return remote(
+            own.at[step, tt, part, at], (upb if up else dnb).at[step, tt, part, at],
+            ch_s.at[step, tt, p], (up_r if up else dn_r).at[step, tt, p],
+            g, h + hp if up else h - hp,
+        )
+
+    def ring_copy(step, part, s, way):
         ref = sbuf.at[step, part, s]
         return remote(
-            ref, ref, rg_s.at[step, part, s], rg_r.at[step, part, s],
-            behind if part else ahead, h,
-        )
-
-    ring_gets = (rel > 0, rel > 0)
-    ring_gives = (rel < n_tgt - 1, rel != 1)
-
-    def sx_copy(step, k, to):
-        return remote(
-            sbuf.at[step, :, 0], sxb.at[step, k], sx_s.at[step, k, to], sx_r.at[step, k],
-            g, g * hp + to,
+            ref, ref, rg_s.at[step, way, part, s], rg_r.at[step, part, s],
+            behind if way else ahead, h,
+        )
+
+    reach = (n_tgt // 2, n_tgt // 2 - 1)
+    ring_gives = [(rel < reach[p], (rel == 0) | (rel >= reach[p] + 2)) for p in range(2)]
+
+    def ring_give(step, s, part, way):
+        @pl.when(ring_gives[part][way])
+        def _():
+            ring_copy(step, part, s, way).start()
+
+    def sx_copy(step, k):
+        return remote(
+            sbuf.at[step, :, 0], sxb.at[step, k], sx_s.at[step, k], sx_r.at[step, k],
+            g, g * hp + k % hp,
+        )
+
+    def sy_copy(step, k, d):
+        return remote(
+            sxb.at[step, k], sxb.at[step, k], sy_s.at[step, k, d], sx_r.at[step, k],
+            g, z * hp + (c + d) % hp,
         )
 
     def band_copy(step, e, sender):
@@ -174,45 +199,62 @@
             (fu_r if up else fd_r).at[q, zz], g, h + hp if up else h - hp,
         )
 
-    def receive_s(step):
-        def one(s):
+    def receive_s(step, s):
+        @pl.when(rel > 0)
+        def _():
             for part in range(2):
-
-                @pl.when(ring_gets[part])
-                def _():
-                    ring_copy(step, part, s).wait_recv()
-
-                    @pl.when(ring_gives[part])
-                    def _():
-                        ring_copy(step, part, s).start()
-
-        loop(sh, one)
+                ring_copy(step, part, s, 0).wait_recv()
+                ring_give(step, s, part, 0)
+                ring_give(step, s, part, 1)
+
         for part in range(2):
-            sends.append(
-                (ring_gives[part], lambda part=part: loop(sh, lambda s: ring_copy(step, part, s).wait_send()))
-            )
+            for way in range(2):
+                sends.append(
+                    (ring_gives[part][way], lambda part=part, way=way: ring_copy(step, part, s, way).wait_send())
+                )
+        if s > 0:
+            return
         for k in range(min(step, n_hist)):
-            for to in range(hp):
-                mine = g * hp + to == h
-
-                @pl.when((h == k) & mine)
-                def _():
-                    sxb[step, k] = sbuf[step, :, 0]
-
-                away = (h == k) & (g * hp + to != h)
-
-                @pl.when(away)
-                def _():
-                    sx_copy(step, k, to).start()
-
-                sends.append((away, lambda k=k, to=to: sx_copy(step, k, to).wait_send()))
+
+            @pl.when((h == k) & root)
+            def _():
+                sxb[step, k] = sbuf[step, :, 0]
+
+            away = (h == k) & (z != g)
+
+            @pl.when(away)
+            def _():
+                sx_copy(step, k).start()
+
+            sends.append((away, lambda k=k: sx_copy(step, k).wait_send()))
+
+    def sums_before_last(step):
+        begin = 0
+        for end in range(max(1, sh - 2), sh):
+            for s in range(begin, end):
+                receive_s(step, s)
+                store_s3(step, s)
+
+            def one(t, begin=begin, end=end):
+                product = dot_of(t, begin, end)
+                acc[t] = acc[t] + product if begin else product
+
+            loop(tt_all, one)
+            begin = end
+        receive_s(step, sh - 1)
+        store_s3(step, sh - 1)
 
     def make_base(step):
         for k in range(min(step, n_hist)):
 
             @pl.when(h != k)
             def _():
-                sx_copy(step, k, 0).wait_recv()
+                sx_copy(step, k).wait_recv()
+
+            @pl.when(c == k % hp)
+            def _():
+                for d in range(1, hp):
+                    sy_copy(step, k, d).start()
 
             store_l3(k + 1, norm * sxb[step, k, 1], -norm * sxb[step, k, 0])
 
@@ -227,42 +269,44 @@
         loop(sh, one)
 
     s_copy.wait()
-    store_s3(0)
+    for s in range(sh):
+        store_s3(0, s)
     pl.semaphore_wait(barrier, n_hist + 1)
 
     for step in range(last):
         if step > 0:
-            receive_s(step)
-            store_s3(step)
-
-        for d in range(1, hp):
-
-            def give(tt, d=d):
+            sums_before_last(step)
+
+        def first_link(tt, step=step):
+            for d in range(1, hp):
+                ex_copy(step, d, tt).wait_recv()
+                own[step, tt] += exr[step, d, tt]
+
+            @pl.when((z < g) & (z == 0))
+            def _():
+                for p in range(PIECES):
+                    chain_copy(step, tt, p, True).start()
+
+            @pl.when((z > g) & (z == nz - 1))
+            def _():
+                for p in range(PIECES):
+                    chain_copy(step, tt, p, False).start()
+
+        def products(tt, step=step):
+            for d in range(1, hp):
                 real, imag = term((c + d) % hp * sh + tt, step)
                 exs[step, d, tt, 0] = real
                 exs[step, d, tt, 1] = imag
                 ex_copy(step, d, tt).start()
-
-            loop(sh, give)
-            sends.append((None, lambda d=d, step=step: loop(sh, lambda tt: ex_copy(step, d, tt).wait_send())))
-
-        def keep(tt):
             real, imag = term(c * sh + tt, step)
             own[step, tt, 0] = real
             own[step, tt, 1] = imag
-            for d in range(1, hp):
-                ex_copy(step, d, tt).wait_recv()
-                own[step, tt] += exr[step, d, tt]
-
-            @pl.when((z < g) & (z == 0))
-            def _():
-                chain_copy(step, tt, True).start()
-
-            @pl.when((z > g) & (z == nz - 1))
-            def _():
-                chain_copy(step, tt, False).start()
-
-        loop(sh, keep)
+            pl.when(tt > 0)(lambda: first_link(tt - 1))
+
+        loop(sh, products)
+        first_link(sh - 1)
+        for d in range(1, hp):
+            sends.append((None, lambda d=d, step=step: loop(sh, lambda tt: ex_copy(step, d, tt).wait_send())))
         if step == 0:
             p_copy.wait()
             r_copy.wait()
@@ -275,23 +319,26 @@
             make_base(step)
 
         def link(tt):
-            @pl.when((z > 0) & (z <= g))
-            def _():
-                chain_copy(step, tt, True).wait_recv()
-                own[step, tt] += upb[step, tt]
-
-            @pl.when((z < nz - 1) & (z >= g))
-            def _():
-                chain_copy(step, tt, False).wait_recv()
-                own[step, tt] += dnb[step, tt]
-
-            @pl.when((z < g) & (z > 0))
-            def _():
-                chain_copy(step, tt, True).start()
-
-            @pl.when((z > g) & (z < nz - 1))
-            def _():
-                chain_copy(step, tt, False).start()
+            for p in range(PIECES):
+                part, at = piece(p)
+
+                @pl.when((z > 0) & (z <= g))
+                def _():
+                    chain_copy(step, tt, p, True).wait_recv()
+                    own[step, tt, part, at] += upb[step, tt, part, at]
+
+                @pl.when((z < nz - 1) & (z >= g))
+                def _():
+                    chain_copy(step, tt, p, False).wait_recv()
+                    own[step, tt, part, at] += dnb[step, tt, part, at]
+
+                @pl.when((z < g) & (z > 0))
+                def _():
+                    chain_copy(step, tt, p, True).start()
+
+                @pl.when((z > g) & (z < nz - 1))
+                def _():
+                    chain_copy(step, tt, p, False).start()
 
             @pl.when(root)
             def _():
@@ -301,17 +348,21 @@
                 factor = -COUPLING * modulus / (1.0 + modulus)
                 sbuf[step + 1, 0, tt] = factor * real
                 sbuf[step + 1, 1, tt] = factor * imag
-                ring_copy(step + 1, 0, tt).start()
-                ring_copy(step + 1, 1, tt).start()
+                for part, way in ((0, 0), (1, 1), (1, 0), (0, 1)):
+                    ring_give(step + 1, tt, part, way)
                 rows[step, 0, tt] = real
                 rows[step, 1, tt] = imag
                 store_x3(step + 1, tt, real, imag)
 
         loop(sh, link)
         for up, gives in ((True, z < g), (False, z > g)):
-            sends.append(
-                (gives, lambda up=up, step=step: loop(sh, lambda tt: chain_copy(step, tt, up).wait_send()))
-            )
+            for p in range(PIECES):
+                sends.append(
+                    (gives, lambda p=p, up=up, step=step: loop(sh, lambda tt: chain_copy(step, tt, p, up).wait_send()))
+                )
+        for k in range(min(step, n_hist)):
+            for d in range(1, hp):
+                sends.append((root & (c == k % hp), lambda k=k, d=d, step=step: sy_copy(step, k, d).wait_send()))
 
         @pl.when(root)
         def _():
@@ -324,8 +375,10 @@
             (root, lambda step=step: loop(n_hist - 1, lambda e: band_copy(step, e + 1, c).wait_send()))
         )
 
-    receive_s(last)
-    store_s3(last)
+    sums_before_last(last)
+    for k in range(min(last, n_hist)):
+        for d in range(1, hp):
+            sends.append((root & (c == k % hp), lambda k=k, d=d: sy_copy(last, k, d).wait_send()))
     pl.when(root)(lambda: make_base(last))
     for q in range(hp):
 
@@ -426,6 +479,7 @@
             vmem((tt, 2, sh, n, n), F32),
             vmem((tt, 3 * sh * n, 2 * n), BF16),
             vmem((2 * n, 3 * sh * n), BF16),
+            vmem((tt, 2 * n, 2 * n), F32),
             vmem((STEPS, 2, sh, n, n), F32),
             vmem((2, tt, n, n), F32),
             vmem((2, n, n), F32),
@@ -449,11 +503,12 @@
             sem((3,)),
             sem((last, hp, sh)),
             sem((last, hp, sh)),
-            sem((last, sh)),
-            sem((last, sh)),
-            sem((last, sh)),
+            sem((last, sh, PIECES)),
+            sem((last, sh, PIECES)),
+            sem((last, sh, PIECES)),
+            sem((STEPS, 2, 2, sh)),
             sem((STEPS, 2, sh)),
-            sem((STEPS, 2, sh)),
+            sem((STEPS, STEPS)),
             sem((STEPS, STEPS, hp)),
             sem((STEPS, STEPS)),
             sem((last, n_hist)),

time: 246 us -> 123 us (0.50); the launches traced: 241 us -> 123 us
  Pallas kernels: 239 us -> 121 us
    pallas_call x1, Pallas kernels: 239 us -> 121 us  [per_device(): pl.pallas_call(functools.partial(kernel, n_tgt, n_hist, norm), out_shape=...]
where the time goes in v2:
time: 123 us
  Pallas kernels  121 us (98%)
  local copies, waits for them, and re-layouts  1.87 us (2%)
    pallas_call x1, Pallas kernels, per_device(): pl.pallas_call(functools.partial(kernel, n_tgt, n_hist, norm), out_shape=...  121 us

profile of v2, /device:TPU:0, one launch (start us, length us, event | category | flops | bytes accessed | tf_op | source)
XLA Modules:
  0.0 122.9 jit_solution(13440728786168426199)
XLA Ops:
  0.0 121.0 %shard_map.46 = f32[4,2,8,16,128]{4,3,2,1,0:T(8,128)} custom-call(f32[2,4,8,128,128]{4,3,2,1,0:T(8,128)} %h_hbm.1, f32[2,4,128,128]{3,2,1,0:T(8,128)} %s_hbm.1, f32[2,8,128,128]{3,2,1,0:T(8,128)} %r_hbm.1, f32[2,128,128]{2,1,0:T(8,128)} %p_hbm.1), custom_call_target="tpu_custom_call" | custom-call | tf_op jit(solution)/shard_map/pallas_call | solution.py:473
  121.0 1.9 %copy.6 = f32[4,2,8,16,128]{4,3,2,1,0:T(8,128)} copy(f32[4,2,8,16,128]{4,3,2,1,0:T(8,128)} %shard_map.46) | data formatting | bytes 1048576

commit v3 on v2

--- a/solution.py
+++ b/solution.py
@@ -11,7 +11,8 @@
 COUPLING = 1.5
 MIXING = 0.7
 MESH = pl.DeviceIdType.MESH
-PIECES = 2
+CUTS = 2
+PIECES = 4
 F32, BF16 = jnp.float32, jnp.bfloat16
 
 
@@ -50,7 +51,7 @@
     rel = (pos - snake(z) + n_tgt) % n_tgt
     ahead, behind = snake((pos + 1) % n_tgt), snake((pos + n_tgt - 1) % n_tgt)
     last = STEPS - 1
-    sends = []
+    sends, bands_sent, older = [], [], []
 
     def remote(src, dst, send_sem, recv_sem, tgt, hist):
         return pltpu.make_async_remote_copy(
@@ -96,6 +97,7 @@
             l3[slot, pl.ds(at, n), pl.ds(n, n)] = high
             l3[slot, pl.ds(at, n), pl.ds(2 * n, n)] = low
 
+    half = sh // 2
     width = 3 * n
 
     def store_s3(step, s):
@@ -130,7 +132,7 @@
             store_h3(t)
             product = dot_of(t, 0, sh)
         else:
-            product = acc[t] + dot_of(t, sh - 1, sh)
+            product = acc[t] + dot_of(t, half, sh)
         real, imag = complex_of(product)
         return (MIXING * norm) * imag, (-MIXING * norm) * real
 
@@ -228,21 +230,27 @@
 
             sends.append((away, lambda k=k: sx_copy(step, k).wait_send()))
 
-    def sums_before_last(step):
-        begin = 0
-        for end in range(max(1, sh - 2), sh):
-            for s in range(begin, end):
-                receive_s(step, s)
-                store_s3(step, s)
-
-            def one(t, begin=begin, end=end):
-                product = dot_of(t, begin, end)
-                acc[t] = acc[t] + product if begin else product
-
-            loop(tt_all, one)
-            begin = end
-        receive_s(step, sh - 1)
-        store_s3(step, sh - 1)
+    def first_sums(step):
+        for s in range(half):
+            receive_s(step, s)
+            store_s3(step, s)
+
+        def one(t):
+            acc[t] = dot_of(t, 0, half)
+
+        loop(tt_all, one)
+        for s in range(half, sh):
+            receive_s(step, s)
+        for s in range(half, sh):
+            store_s3(step, s)
+
+    def flush(waits):
+        for gives, wait in waits:
+            if gives is None:
+                wait()
+            else:
+                pl.when(gives)(wait)
+        waits.clear()
 
     def make_base(step):
         for k in range(min(step, n_hist)):
@@ -275,7 +283,10 @@
 
     for step in range(last):
         if step > 0:
-            sums_before_last(step)
+            flush(sends)
+            flush(older)
+            older, bands_sent = bands_sent, []
+            first_sums(step)
 
         def first_link(tt, step=step):
             for d in range(1, hp):
@@ -371,82 +382,83 @@
             ]
             loop(n_hist - 1, lambda e: band_copy(step, e + 1, c).start())
 
-        sends.append(
+        bands_sent.append(
             (root, lambda step=step: loop(n_hist - 1, lambda e: band_copy(step, e + 1, c).wait_send()))
         )
 
-    sums_before_last(last)
+    flush(sends)
+    flush(older)
+    first_sums(last)
     for k in range(min(last, n_hist)):
         for d in range(1, hp):
             sends.append((root & (c == k % hp), lambda k=k, d=d: sy_copy(last, k, d).wait_send()))
     pl.when(root)(lambda: make_base(last))
-    for q in range(hp):
-
-        def bands(tt, q=q):
-            for part, value in enumerate(term(q * sh + tt, last)):
-                for b in range(n_hist):
-                    fin[q, b // hp, b % hp, tt, part] = value[b * band : (b + 1) * band]
-
-        loop(sh, bands)
-
-        @pl.when(root & (c == q))
-        def _():
-            def add(tt):
-                for part in range(2):
-                    for b in range(n_hist):
-                        fin[q, b // hp, b % hp, tt, part] += base[tt, part, pl.ds(b * band, band)]
-
-            loop(sh, add)
-
-        for d in range(1, hp):
-            fin_ex_copy(q, d).start()
-            sends.append((None, lambda q=q, d=d: fin_ex_copy(q, d).wait_send()))
-
-    for q in range(hp):
-        for d in range(1, hp):
-            fin_ex_copy(q, d).wait_recv()
-
-        def both(zz, q=q):
-            value = fin[q, zz, c]
-            for d in range(1, hp):
-                value += exf[q, d, zz]
-            fsum[q, zz] = value
-
-        loop(nz, both)
+    n_cut, su = fin.shape[0], fin.shape[3]
+    per_core = n_cut // hp
+
+    def far(u, go):
         for dist in range(nz - 1, 0, -1):
             for up in (True, False):
                 zz = z + dist if up else z - dist
                 on_way = zz < nz if up else zz >= 0
-                first = z == 0 if up else z == nz - 1
-
-                @pl.when(on_way)
-                def _():
-                    @pl.when(jnp.logical_not(first))
-                    def _():
-                        fin_chain_copy(q, zz, up).wait_recv()
-                        fsum[q, zz] += (upf if up else dnf)[q, zz]
-
-                    fin_chain_copy(q, zz, up).start()
-
-                sends.append(
-                    (on_way, lambda q=q, zz=zz, up=up: fin_chain_copy(q, zz, up).wait_send())
-                )
-    for q in range(hp):
-
-        @pl.when(z > 0)
-        def _():
-            fin_chain_copy(q, z, True).wait_recv()
-            fsum[q, z] += upf[q, z]
-
-        @pl.when(z < nz - 1)
-        def _():
-            fin_chain_copy(q, z, False).wait_recv()
-            fsum[q, z] += dnf[q, z]
-
-        for tt in range(sh):
-            for part in range(2):
-                out_ref[last, part, q * sh + tt] = fsum[q, z, tt, part]
-
+                go(u, zz, up, on_way, z == 0 if up else z == nz - 1)
+
+    def far_first(u, zz, up, on_way, first):
+        @pl.when(on_way & first)
+        def _():
+            fin_chain_copy(u, zz, up).start()
+
+    def far_next(u, zz, up, on_way, first):
+        @pl.when(on_way & jnp.logical_not(first))
+        def _():
+            fin_chain_copy(u, zz, up).wait_recv()
+            fsum[u, zz] += (upf if up else dnf)[u, zz]
+            fin_chain_copy(u, zz, up).start()
+
+        sends.append((on_way, lambda: fin_chain_copy(u, zz, up).wait_send()))
+
+    def of_pair(u):
+        for d in range(1, hp):
+            fin_ex_copy(u, d).wait_recv()
+
+        def both(zz):
+            value = fin[u, zz, c]
+            for d in range(1, hp):
+                value += exf[u, d, zz]
+            fsum[u, zz] = value
+
+        loop(nz, both)
+        far(u, far_first)
+
+    for u in range(n_cut):
+
+        def bands(i, u=u):
+            for part, value in enumerate(term(u * su + i, last)):
+                for b in range(n_hist):
+                    fin[u, b // hp, b % hp, i, part] = value[b * band : (b + 1) * band]
+
+        loop(su, bands)
+
+        @pl.when(root & (c == u // per_core))
+        def _():
+            def add(i):
+                for part in range(2):
+                    for b in range(n_hist):
+                        fin[u, b // hp, b % hp, i, part] += base[
+                            u % per_core * su + i, part, pl.ds(b * band, band)
+                        ]
+
+            loop(su, add)
+
+        for d in range(1, hp):
+            fin_ex_copy(u, d).start()
+            sends.append((None, lambda u=u, d=d: fin_ex_copy(u, d).wait_send()))
+        if u > 0:
+            of_pair(u - 1)
+    of_pair(n_cut - 1)
+
+    for u in range(n_cut):
+        far(u, far_next)
     for step in range(last):
         for sender in range(hp):
 
@@ -455,12 +467,24 @@
                 band_copy(step, 1, sender).wait_recv()
 
         out_ref[step] = outb[step]
-
-    for gives, wait in sends:
-        if gives is None:
-            wait()
-        else:
-            pl.when(gives)(wait)
+    for u in range(n_cut):
+
+        @pl.when(z > 0)
+        def _():
+            fin_chain_copy(u, z, True).wait_recv()
+            fsum[u, z] += upf[u, z]
+
+        @pl.when(z < nz - 1)
+        def _():
+            fin_chain_copy(u, z, False).wait_recv()
+            fsum[u, z] += dnf[u, z]
+
+        for i in range(su):
+            for part in range(2):
+                out_ref[last, part, u * su + i] = fsum[u, z, i, part]
+
+    flush(bands_sent)
+    flush(sends)
 
 
 def per_device(history, self_energy, green_row, propagator):
@@ -469,6 +493,8 @@
     hp, band, last = n_hist // n_tgt, n // n_hist, STEPS - 1
     nz = n_hist // hp
     norm = float(sh * n_hist * n) ** (-0.5)
+    n_cut = hp * CUTS
+    su = tt // n_cut
     vmem, sem = pltpu.VMEM, pltpu.SemaphoreType.DMA
     return pl.pallas_call(
         functools.partial(kernel, n_tgt, n_hist, norm),
@@ -494,11 +520,11 @@
             vmem((STEPS, STEPS, 2, n, n), F32),
             vmem((STEPS, 2 * n, 3 * n), BF16),
             vmem((last, 2, tt, band, n), F32),
-            vmem((hp, nz, hp, sh, 2, band, n), F32),
-            vmem((hp, hp, nz, sh, 2, band, n), F32),
-            vmem((hp, nz, sh, 2, band, n), F32),
-            vmem((hp, nz, sh, 2, band, n), F32),
-            vmem((hp, nz, sh, 2, band, n), F32),
+            vmem((n_cut, nz, hp, su, 2, band, n), F32),
+            vmem((n_cut, hp, nz, su, 2, band, n), F32),
+            vmem((n_cut, nz, su, 2, band, n), F32),
+            vmem((n_cut, nz, su, 2, band, n), F32),
+            vmem((n_cut, nz, su, 2, band, n), F32),
             sem((tt,)),
             sem((3,)),
             sem((last, hp, sh)),
@@ -513,11 +539,11 @@
             sem((STEPS, STEPS)),
             sem((last, n_hist)),
             sem((last, hp)),
-            sem((hp, hp)),
-            sem((hp, hp)),
-            sem((hp, nz)),
-            sem((hp, nz)),
-            sem((hp, nz)),
+            sem((n_cut, hp)),
+            sem((n_cut, hp)),
+            sem((n_cut, nz)),
+            sem((n_cut, nz)),
+            sem((n_cut, nz)),
         ],
         compiler_params=pltpu.CompilerParams(
             collective_id=0, has_side_effects=True, vmem_limit_bytes=56 * 2**20

time: 123 us -> 122 us (level)
  no operation moved by 1% of the time
where the time goes in v3:
time: 122 us
  Pallas kernels  120 us (98%)
  local copies, waits for them, and re-layouts  1.87 us (2%)
    pallas_call x1, Pallas kernels, per_device(): pl.pallas_call(functools.partial(kernel, n_tgt, n_hist, norm), out_shape=...  120 us

profile of v3, /device:TPU:0, one launch (start us, length us, event | category | flops | bytes accessed | tf_op | source)
XLA Modules:
  0.0 121.9 jit_solution(11105622920816748934)
XLA Ops:
  0.0 120.0 %shard_map.46 = f32[4,2,8,16,128]{4,3,2,1,0:T(8,128)} custom-call(f32[2,4,8,128,128]{4,3,2,1,0:T(8,128)} %h_hbm.1, f32[2,4,128,128]{3,2,1,0:T(8,128)} %s_hbm.1, f32[2,8,128,128]{3,2,1,0:T(8,128)} %r_hbm.1, f32[2,128,128]{2,1,0:T(8,128)} %p_hbm.1), custom_call_target="tpu_custom_call" | custom-call | tf_op jit(solution)/shard_map/pallas_call | solution.py:499
  120.0 1.9 %copy.6 = f32[4,2,8,16,128]{4,3,2,1,0:T(8,128)} copy(f32[4,2,8,16,128]{4,3,2,1,0:T(8,128)} %shard_map.46) | data formatting | bytes 1048576

commit v4 on v3

--- a/solution.py
+++ b/solution.py
@@ -143,31 +143,32 @@
         )
 
     def piece(p):
-        per_part = PIECES // 2
-        return p // per_part, pl.ds(p % per_part * (n // per_part), n // per_part)
+        return pl.ds(p * (n // PIECES), n // PIECES)
 
     def chain_copy(step, tt, p, up):
-        part, at = piece(p)
-        return remote(
-            own.at[step, tt, part, at], (upb if up else dnb).at[step, tt, part, at],
+        at = piece(p)
+        return remote(
+            own.at[step, tt, :, at], (upb if up else dnb).at[step, tt, :, at],
             ch_s.at[step, tt, p], (up_r if up else dn_r).at[step, tt, p],
             g, h + hp if up else h - hp,
         )
 
-    def ring_copy(step, part, s, way):
-        ref = sbuf.at[step, part, s]
-        return remote(
-            ref, ref, rg_s.at[step, way, part, s], rg_r.at[step, part, s],
+    def ring_copy(step, p, s, way):
+        ref = sbuf.at[step, :, s, piece(p)]
+        return remote(
+            ref, ref, rg_s.at[step, way, p, s], rg_r.at[step, p, s],
             behind if way else ahead, h,
         )
 
     reach = (n_tgt // 2, n_tgt // 2 - 1)
-    ring_gives = [(rel < reach[p], (rel == 0) | (rel >= reach[p] + 2)) for p in range(2)]
-
-    def ring_give(step, s, part, way):
-        @pl.when(ring_gives[part][way])
-        def _():
-            ring_copy(step, part, s, way).start()
+    ring_gives = [(rel < reach[p], (rel == 0) | (rel >= reach[p] + 2)) for p in range(2)] * (PIECES // 2)
+
+    def ring_give(step, s, p):
+        for way in (p % 2, 1 - p % 2):
+
+            @pl.when(ring_gives[p][way])
+            def _():
+                ring_copy(step, p, s, way).start()
 
     def sx_copy(step, k):
         return remote(
@@ -204,15 +205,14 @@
     def receive_s(step, s):
         @pl.when(rel > 0)
         def _():
-            for part in range(2):
-                ring_copy(step, part, s, 0).wait_recv()
-                ring_give(step, s, part, 0)
-                ring_give(step, s, part, 1)
-
-        for part in range(2):
+            for p in range(PIECES):
+                ring_copy(step, p, s, 0).wait_recv()
+                ring_give(step, s, p)
+
+        for p in range(PIECES):
             for way in range(2):
                 sends.append(
-                    (ring_gives[part][way], lambda part=part, way=way: ring_copy(step, part, s, way).wait_send())
+                    (ring_gives[p][way], lambda p=p, way=way: ring_copy(step, p, s, way).wait_send())
                 )
         if s > 0:
             return
@@ -235,10 +235,12 @@
             receive_s(step, s)
             store_s3(step, s)
 
-        def one(t):
-            acc[t] = dot_of(t, 0, half)
-
-        loop(tt_all, one)
+        def one(i):
+            pair = [dot_of(2 * i + j, 0, half) for j in range(2)]
+            for j in range(2):
+                acc[2 * i + j] = pair[j]
+
+        loop(tt_all // 2, one)
         for s in range(half, sh):
             receive_s(step, s)
         for s in range(half, sh):
@@ -304,14 +306,11 @@
                     chain_copy(step, tt, p, False).start()
 
         def products(tt, step=step):
+            terms = [term((c + d) % hp * sh + tt, step) for d in [*range(1, hp), 0]]
             for d in range(1, hp):
-                real, imag = term((c + d) % hp * sh + tt, step)
-                exs[step, d, tt, 0] = real
-                exs[step, d, tt, 1] = imag
+                exs[step, d, tt, 0], exs[step, d, tt, 1] = terms[d - 1]
                 ex_copy(step, d, tt).start()
-            real, imag = term(c * sh + tt, step)
-            own[step, tt, 0] = real
-            own[step, tt, 1] = imag
+            own[step, tt, 0], own[step, tt, 1] = terms[hp - 1]
             pl.when(tt > 0)(lambda: first_link(tt - 1))
 
         loop(sh, products)
@@ -331,17 +330,17 @@
 
         def link(tt):
             for p in range(PIECES):
-                part, at = piece(p)
+                at = piece(p)
 
                 @pl.when((z > 0) & (z <= g))
                 def _():
                     chain_copy(step, tt, p, True).wait_recv()
-                    own[step, tt, part, at] += upb[step, tt, part, at]
+                    own[step, tt, :, at] += upb[step, tt, :, at]
 
                 @pl.when((z < nz - 1) & (z >= g))
                 def _():
                     chain_copy(step, tt, p, False).wait_recv()
-                    own[step, tt, part, at] += dnb[step, tt, part, at]
+                    own[step, tt, :, at] += dnb[step, tt, :, at]
 
                 @pl.when((z < g) & (z > 0))
                 def _():
@@ -351,19 +350,21 @@
                 def _():
                     chain_copy(step, tt, p, False).start()
 
+                @pl.when(root)
+                def _():
+                    real = own[step, tt, 0, at] + base[tt, 0, at]
+                    imag = own[step, tt, 1, at] + base[tt, 1, at]
+                    modulus = real * real + imag * imag
+                    factor = -COUPLING * modulus / (1.0 + modulus)
+                    sbuf[step + 1, 0, tt, at] = factor * real
+                    sbuf[step + 1, 1, tt, at] = factor * imag
+                    ring_give(step + 1, tt, p)
+                    rows[step, 0, tt, at] = real
+                    rows[step, 1, tt, at] = imag
+
             @pl.when(root)
             def _():
-                real = own[step, tt, 0] + base[tt, 0]
-                imag = own[step, tt, 1] + base[tt, 1]
-                modulus = real * real + imag * imag
-                factor = -COUPLING * modulus / (1.0 + modulus)
-                sbuf[step + 1, 0, tt] = factor * real
-                sbuf[step + 1, 1, tt] = factor * imag
-                for part, way in ((0, 0), (1, 1), (1, 0), (0, 1)):
-                    ring_give(step + 1, tt, part, way)
-                rows[step, 0, tt] = real
-                rows[step, 1, tt] = imag
-                store_x3(step + 1, tt, real, imag)
+                store_x3(step + 1, tt, rows[step, 0, tt], rows[step, 1, tt])
 
         loop(sh, link)
         for up, gives in ((True, z < g), (False, z > g)):
@@ -532,8 +533,8 @@
             sem((last, sh, PIECES)),
             sem((last, sh, PIECES)),
             sem((last, sh, PIECES)),
-            sem((STEPS, 2, 2, sh)),
-            sem((STEPS, 2, sh)),
+            sem((STEPS, 2, PIECES, sh)),
+            sem((STEPS, PIECES, sh)),
             sem((STEPS, STEPS)),
             sem((STEPS, STEPS, hp)),
             sem((STEPS, STEPS)),

time: 122 us -> 117 us (0.959)
  Pallas kernels: 120 us -> 115 us
    pallas_call x1, Pallas kernels: 120 us -> 115 us  [per_device(): pl.pallas_call(functools.partial(kernel, n_tgt, n_hist, norm), out_shape=...]
where the time goes in v4:
time: 117 us
  Pallas kernels  115 us (98%)
  local copies, waits for them, and re-layouts  1.87 us (2%)
    pallas_call x1, Pallas kernels, per_device(): pl.pallas_call(functools.partial(kernel, n_tgt, n_hist, norm), out_shape=...  115 us

profile of v4, /device:TPU:0, one launch (start us, length us, event | category | flops | bytes accessed | tf_op | source)
XLA Modules:
  0.0 116.7 jit_solution(16409699968257494446)
XLA Ops:
  0.0 114.8 %shard_map.46 = f32[4,2,8,16,128]{4,3,2,1,0:T(8,128)} custom-call(f32[2,4,8,128,128]{4,3,2,1,0:T(8,128)} %h_hbm.1, f32[2,4,128,128]{3,2,1,0:T(8,128)} %s_hbm.1, f32[2,8,128,128]{3,2,1,0:T(8,128)} %r_hbm.1, f32[2,128,128]{2,1,0:T(8,128)} %p_hbm.1), custom_call_target="tpu_custom_call" | custom-call | tf_op jit(solution)/shard_map/pallas_call | solution.py:500
  114.9 1.9 %copy.6 = f32[4,2,8,16,128]{4,3,2,1,0:T(8,128)} copy(f32[4,2,8,16,128]{4,3,2,1,0:T(8,128)} %shard_map.46) | data formatting | bytes 1048576

commit v5 on v4

v5 whole, which is shorter than its diff:
```python
import functools

import jax
import jax.numpy as jnp
from jax import lax
from jax.experimental import pallas as pl
from jax.experimental.pallas import tpu as pltpu
from jax.sharding import PartitionSpec as P

STEPS = 4
COUPLING = 1.5
MIXING = 0.7
MESH = pl.DeviceIdType.MESH
CUTS = 2
PIECES = 4
F32, BF16 = jnp.float32, jnp.bfloat16


def split(value):
    high = value.astype(BF16)
    return high, (value - high.astype(F32)).astype(BF16)


def complex_of(product):
    n = product.shape[0] // 2
    return product[:n, :n] - product[n:, n:], product[:n, n:] + product[n:, :n]


def snake(index):
    q, r = index // 2, index % 2
    return 2 * q + r + (q % 2) * (1 - 2 * r)


def kernel(
    n_tgt, n_hist, norm,
    h_hbm, s_hbm, r_hbm, p_hbm, out_ref,
    hst, h3, s3, acc, sbuf, total, rin, pin, exs, exr, own, upb, dnb, rows, x3, base, sxb, l3, outb,
    fin, exf, fsum, upf, dnf,
    h_sem, in_sem, ex_s, ex_r, ch_s, up_r, dn_r, rg_s, rg_r, sx_s, sy_s, sx_r, bd_s, bd_r,
    fx_s, fx_r, fc_s, fu_r, fd_r,
):
    _, sh, tt_all, n, _ = h_hbm.shape
    hp = n_hist // n_tgt
    nz = n_hist // hp
    band = n // n_hist
    depth = sh * n
    g, h = lax.axis_index("tgt"), lax.axis_index("hist")
    z, c = h // hp, h % hp
    root = z == g
    pos = snake(g)
    rel = (pos - snake(z) + n_tgt) % n_tgt
    ahead, behind = snake((pos + 1) % n_tgt), snake((pos + n_tgt - 1) % n_tgt)
    last = STEPS - 1

    def remote(src, dst, send_sem, recv_sem, tgt, hist):
        return pltpu.make_async_remote_copy(
            src_ref=src, dst_ref=dst, send_sem=send_sem, recv_sem=recv_sem,
            device_id={"tgt": tgt, "hist": hist}, device_id_type=MESH,
        )

    def loop(count, body):
        lax.fori_loop(0, count, lambda i, _: (body(i), None)[1], None)

    def turn(i):
        tt, d = i // hp, (i % hp + 1) % hp
        return tt, d, (c + d) % hp * sh + tt

    def h_copy(t):
        return pltpu.make_async_copy(h_hbm.at[:, :, t], hst.at[t], h_sem.at[t])

    s_copy = pltpu.make_async_copy(s_hbm, sbuf.at[0], in_sem.at[0])
    p_copy = pltpu.make_async_copy(p_hbm, pin, in_sem.at[1])
    r_copy = pltpu.make_async_copy(r_hbm, rin, in_sem.at[2])
    s_copy.start()
    loop(tt_all, lambda i: h_copy(turn(i)[2]).start())
    p_copy.start()
    r_copy.start()

    barrier = pltpu.get_barrier_semaphore()
    for e in range(1, n_hist):
        pl.semaphore_signal(
            barrier, inc=1, device_id={"tgt": g, "hist": (h + e) % n_hist}, device_id_type=MESH
        )
    for near in (ahead, behind):
        pl.semaphore_signal(barrier, inc=1, device_id={"tgt": near, "hist": h}, device_id_type=MESH)

    def store_x3(slot, tt, real, imag):
        for at, value in ((0, real), (n, imag)):
            high, low = split(value)
            cols = pl.ds(at, n)
            x3[slot, tt, pl.ds(0, n), cols] = high
            x3[slot, tt, pl.ds(n, n), cols] = low
            x3[slot, tt, pl.ds(2 * n, n), cols] = high

    def store_l3(slot, real, imag):
        for at, value in ((0, real), (n, imag)):
            high, low = split(value)
            l3[slot, pl.ds(at, n), pl.ds(0, n)] = high
            l3[slot, pl.ds(at, n), pl.ds(n, n)] = high
            l3[slot, pl.ds(at, n), pl.ds(2 * n, n)] = low

    half = sh // 2
    width = 3 * n

    def store_s3(step, s):
        for part in range(2):
            high, low = split(sbuf[step, part, s])
            r = pl.ds(part * n, n)
            s3[r, pl.ds(s * width, n)] = high
            s3[r, pl.ds(s * width + n, n)] = high
            s3[r, pl.ds(s * width + 2 * n, n)] = low
        if s == 0:

            @pl.when(h < step)
            def _():
                s3[:, pl.ds(0, width)] = jnp.zeros((2 * n, width), BF16)

    def store_h3(t):
        h_copy(t).wait()
        for s in range(sh):
            for part in range(2):
                high, low = split(hst[t, part, s])
                cols = pl.ds(part * n, n)
                h3[t, pl.ds(s * width, n), cols] = high
                h3[t, pl.ds(s * width + n, n), cols] = low
                h3[t, pl.ds(s * width + 2 * n, n), cols] = high

    def dot_of(t, begin, end):
        at = pl.ds(begin * width, (end - begin) * width)
        return jnp.dot(s3[:, at], h3[t, at, :], preferred_element_type=F32)

    def term(t):
        real, imag = complex_of(acc[t] + dot_of(t, half, sh))
        return (MIXING * norm) * imag, (-MIXING * norm) * real

    def ex_copy(step, d, tt):
        return remote(
            exs.at[step, d, tt], exr.at[step, d, tt], ex_s.at[step, d, tt], ex_r.at[step, d, tt],
            g, z * hp + (c + d) % hp,
        )

    def piece(p):
        return pl.ds(p * (n // PIECES), n // PIECES)

    def chain_copy(step, tt, p, up):
        at = piece(p)
        return remote(
            own.at[step, tt, :, at], (upb if up else dnb).at[step, tt, :, at],
            ch_s.at[step, tt, p], (up_r if up else dn_r).at[step, tt, p],
            g, h + hp if up else h - hp,
        )

    def ring_copy(step, p, s, way):
        ref = sbuf.at[step, :, s, piece(p)]
        return remote(
            ref, ref, rg_s.at[step, way, p, s], rg_r.at[step, p, s],
            behind if way else ahead, h,
        )

    reach = (n_tgt // 2, n_tgt // 2 - 1)
    ring_gives = [(rel < reach[p], (rel == 0) | (rel >= reach[p] + 2)) for p in range(2)] * (PIECES // 2)

    def ring_give(step, s, p):
        for way in (p % 2, 1 - p % 2):

            @pl.when(ring_gives[p][way])
            def _():
                ring_copy(step, p, s, way).start()

    def sx_copy(step, k):
        return remote(
            sbuf.at[step, :, 0], sxb.at[step, k], sx_s.at[step, k], sx_r.at[step, k],
            g, g * hp + k % hp,
        )

    def sy_copy(step, k, d):
        return remote(
            sxb.at[step, k], sxb.at[step, k], sy_s.at[step, k, d], sx_r.at[step, k],
            g, z * hp + (c + d) % hp,
        )

    def band_copy(step, e, sender):
        to = (h + e) % n_hist
        return remote(
            rows.at[step, :, :, pl.ds(pl.multiple_of(to * band, band), band)],
            outb.at[step, :, pl.ds(sender * sh, sh)], bd_s.at[step, e], bd_r.at[step, sender],
            g, to,
        )

    def fin_ex_copy(q, d):
        to = (c + d) % hp
        return remote(
            fin.at[q, :, to], exf.at[q, d], fx_s.at[q, d], fx_r.at[q, d], g, z * hp + to
        )

    def fin_chain_copy(q, zz, up):
        return remote(
            fsum.at[q, zz], (upf if up else dnf).at[q, zz], fc_s.at[q, zz],
            (fu_r if up else fd_r).at[q, zz], g, h + hp if up else h - hp,
        )

    def receive_s(step, s):
        @pl.when((rel > 0) & (step > 0))
        def _():
            for p in range(PIECES):
                ring_copy(step, p, s, 0).wait_recv()
                ring_give(step, s, p)

        if s == 0:

            @pl.when((h < step) & root)
            def _():
                sxb[step, h] = sbuf[step, :, 0]

            @pl.when((h < step) & (z != g))
            def _():
                sx_copy(step, h).start()

    def make_base(step):
        def slot(k):
            @pl.when(h != k)
            def _():
                sx_copy(step, k).wait_recv()

            @pl.when(c == k % hp)
            def _():
                for d in range(1, hp):
                    sy_copy(step, k, d).start()

            store_l3(k + 1, norm * sxb[step, k, 1], -norm * sxb[step, k, 0])

        loop(step, slot)

        def one(tt):
            total[...] = jnp.dot(l3[0], x3[step, tt], preferred_element_type=F32)

            def add(k):
                total[...] += jnp.dot(l3[k + 1], x3[k + 1, tt], preferred_element_type=F32)

            loop(step, add)
            real, imag = complex_of(total[...])
            base[tt, 0] = MIXING * real
            base[tt, 1] = MIXING * imag

        loop(sh, one)

    def sent(step):
        for p in range(PIECES):
            for way in range(2):

                @pl.when(ring_gives[p][way])
                def _():
                    loop(sh, lambda s: ring_copy(step, p, s, way).wait_send())

        @pl.when((h < step) & (z != g))
        def _():
            sx_copy(step, h).wait_send()

        @pl.when(root)
        def _():
            def slot(k):
                @pl.when(c == k % hp)
                def _():
                    for d in range(1, hp):
                        sy_copy(step, k, d).wait_send()

            loop(step, slot)

    def sums_sent(step):
        for d in range(1, hp):
            loop(sh, lambda tt: ex_copy(step, d, tt).wait_send())
        for up, gives in ((True, z < g), (False, z > g)):

            @pl.when(gives)
            def _():
                for p in range(PIECES):
                    loop(sh, lambda tt: chain_copy(step, tt, p, up).wait_send())

    def bands_sent(step):
        @pl.when(root)
        def _():
            loop(n_hist - 1, lambda e: band_copy(step, e + 1, c).wait_send())

    n_cut, su = fin.shape[0], fin.shape[3]
    per_core = n_cut // hp

    def first_link(step, tt):
        for d in range(1, hp):
            ex_copy(step, d, tt).wait_recv()
            own[step, tt] += exr[step, d, tt]

        @pl.when((z < g) & (z == 0))
        def _():
            for p in range(PIECES):
                chain_copy(step, tt, p, True).start()

        @pl.when((z > g) & (z == nz - 1))
        def _():
            for p in range(PIECES):
                chain_copy(step, tt, p, False).start()

    def link(step, tt):
        for p in range(PIECES):
            at = piece(p)

            @pl.when((z > 0) & (z <= g))
            def _():
                chain_copy(step, tt, p, True).wait_recv()
                own[step, tt, :, at] += upb[step, tt, :, at]

            @pl.when((z < nz - 1) & (z >= g))
            def _():
                chain_copy(step, tt, p, False).wait_recv()
                own[step, tt, :, at] += dnb[step, tt, :, at]

            @pl.when((z < g) & (z > 0))
            def _():
                chain_copy(step, tt, p, True).start()

            @pl.when((z > g) & (z < nz - 1))
            def _():
                chain_copy(step, tt, p, False).start()

            @pl.when(root)
            def _():
                real = own[step, tt, 0, at] + base[tt, 0, at]
                imag = own[step, tt, 1, at] + base[tt, 1, at]
                modulus = real * real + imag * imag
                factor = -COUPLING * modulus / (1.0 + modulus)
                sbuf[step + 1, 0, tt, at] = factor * real
                sbuf[step + 1, 1, tt, at] = factor * imag
                ring_give(step + 1, tt, p)
                rows[step, 0, tt, at] = real
                rows[step, 1, tt, at] = imag

        @pl.when(root)
        def _():
            store_x3(step + 1, tt, rows[step, 0, tt], rows[step, 1, tt])

    def far(u, go):
        for dist in range(nz - 1, 0, -1):
            for up in (True, False):
                zz = z + dist if up else z - dist
                on_way = zz < nz if up else zz >= 0
                go(u, zz, up, on_way, z == 0 if up else z == nz - 1)

    def far_first(u, zz, up, on_way, first):
        @pl.when(on_way & first)
        def _():
            fin_chain_copy(u, zz, up).start()

    def far_next(u, zz, up, on_way, first):
        @pl.when(on_way & jnp.logical_not(first))
        def _():
            fin_chain_copy(u, zz, up).wait_recv()
            fsum[u, zz] += (upf if up else dnf)[u, zz]
            fin_chain_copy(u, zz, up).start()

    def far_sent(u, zz, up, on_way, first):
        @pl.when(on_way)
        def _():
            fin_chain_copy(u, zz, up).wait_send()

    def of_pair(u):
        for d in range(1, hp):
            fin_ex_copy(u, d).wait_recv()
        for zz in range(nz):
            value = fin[u, zz, c]
            for d in range(1, hp):
                value += exf[u, d, zz]
            fsum[u, zz] = value
        far(u, far_first)

    def product(step, i):
        tt, d, t = turn(i)
        is_last = step // last
        t = is_last * i + (1 - is_last) * t

        @pl.when(step == 0)
        def _():
            store_h3(t)
            acc[t] = dot_of(t, 0, half)

        real, imag = term(t)

        @pl.when((step < last) & (d > 0))
        def _():
            exs[step, d, tt, 0], exs[step, d, tt, 1] = real, imag
            ex_copy(step, d, tt).start()

        @pl.when((step < last) & (d == 0))
        def _():
            own[step, tt, 0], own[step, tt, 1] = real, imag
            pl.when(tt > 0)(lambda: first_link(step, tt - 1))

        @pl.when(step == last)
        def _():
            u, r = i // su, i % su
            for part, value in enumerate((real, imag)):
                for b in range(n_hist):
                    fin[u, b // hp, b % hp, r, part] = value[b * band : (b + 1) * band]

            @pl.when(root & (c == u // per_core))
            def _():
                for part in range(2):
                    for b in range(n_hist):
                        fin[u, b // hp, b % hp, r, part] += base[
                            u % per_core * su + r, part, pl.ds(b * band, band)
                        ]

            @pl.when(r == su - 1)
            def _():
                for d in range(1, hp):
                    fin_ex_copy(u, d).start()
                pl.when(u > 0)(lambda: of_pair(u - 1))

    def run(step):
        @pl.when(step > 0)
        def _():
            sums_sent(step - 1)

        @pl.when(step > 1)
        def _():
            sent(step - 1)
            bands_sent(step - 2)

        for s in range(half):
            receive_s(step, s)
            store_s3(step, s)

        @pl.when(step > 0)
        def _():
            def one(t):
                acc[t] = dot_of(t, 0, half)

            loop(tt_all, one)

        for s in range(half, sh):
            receive_s(step, s)
            store_s3(step, s)
        pl.when(root)(lambda: make_base(step))
        loop(tt_all, lambda i: product(step, i))

        @pl.when(step < last)
        def _():
            first_link(step, sh - 1)
            loop(sh, lambda tt: link(step, tt))

            @pl.when(root)
            def _():
                outb[step, :, pl.ds(c * sh, sh)] = rows[
                    step, :, :, pl.ds(pl.multiple_of(h * band, band), band)
                ]
                loop(n_hist - 1, lambda e: band_copy(step, e + 1, c).start())

    s_copy.wait()
    p_copy.wait()
    r_copy.wait()

    @pl.when(root)
    def _():
        store_l3(0, pin[0], pin[1])
        loop(sh, lambda tt: store_x3(0, tt, rin[0, c * sh + tt], rin[1, c * sh + tt]))

    pl.semaphore_wait(barrier, n_hist + 1)
    loop(STEPS, run)

    of_pair(n_cut - 1)
    loop(n_cut, lambda u: far(u, far_next))
    for step in range(last):
        for sender in range(hp):

            @pl.when(h != g * hp + sender)
            def _():
                band_copy(step, 1, sender).wait_recv()

        out_ref[step] = outb[step]
    sent(last)
    bands_sent(last - 1)

    def finish(u):
        @pl.when(z > 0)
        def _():
            fin_chain_copy(u, z, True).wait_recv()
            fsum[u, z] += upf[u, z]

        @pl.when(z < nz - 1)
        def _():
            fin_chain_copy(u, z, False).wait_recv()
            fsum[u, z] += dnf[u, z]

        for i in range(su):
            for part in range(2):
                out_ref[last, part, u * su + i] = fsum[u, z, i, part]

    loop(n_cut, finish)

    def finish_sent(u):
        for d in range(1, hp):
            fin_ex_copy(u, d).wait_send()
        far(u, far_sent)

    loop(n_cut, finish_sent)


def per_device(history, self_energy, green_row, propagator):
    n_tgt, n_hist = lax.axis_size("tgt"), lax.axis_size("hist")
    _, sh, tt, n, _ = history.shape
    hp, band, last = n_hist // n_tgt, n // n_hist, STEPS - 1
    nz = n_hist // hp
    norm = float(sh * n_hist * n) ** (-0.5)
    n_cut = hp * CUTS
    su = tt // n_cut
    vmem, sem = pltpu.VMEM, pltpu.SemaphoreType.DMA
    return pl.pallas_call(
        functools.partial(kernel, n_tgt, n_hist, norm),
        out_shape=jax.ShapeDtypeStruct((STEPS, 2, tt, band, n), F32),
        in_specs=[pl.BlockSpec(memory_space=pl.ANY)] * 4,
        out_specs=pl.BlockSpec(memory_space=pltpu.VMEM),
        scratch_shapes=[
            vmem((tt, 2, sh, n, n), F32),
            vmem((tt, 3 * sh * n, 2 * n), BF16),
            vmem((2 * n, 3 * sh * n), BF16),
            vmem((tt, 2 * n, 2 * n), F32),
            vmem((STEPS, 2, sh, n, n), F32),
            vmem((2 * n, 2 * n), F32),
            vmem((2, tt, n, n), F32),
            vmem((2, n, n), F32),
            vmem((last, hp, sh, 2, n, n), F32),
            vmem((last, hp, sh, 2, n, n), F32),
            vmem((last, sh, 2, n, n), F32),
            vmem((last, sh, 2, n, n), F32),
            vmem((last, sh, 2, n, n), F32),
            vmem((last, 2, sh, n, n), F32),
            vmem((STEPS, sh, 3 * n, 2 * n), BF16),
            vmem((sh, 2, n, n), F32),
            vmem((STEPS, STEPS, 2, n, n), F32),
            vmem((STEPS, 2 * n, 3 * n), BF16),
            vmem((last, 2, tt, band, n), F32),
            vmem((n_cut, nz, hp, su, 2, band, n), F32),
            vmem((n_cut, hp, nz, su, 2, band, n), F32),
            vmem((n_cut, nz, su, 2, band, n), F32),
            vmem((n_cut, nz, su, 2, band, n), F32),
            vmem((n_cut, nz, su, 2, band, n), F32),
            sem((tt,)),
            sem((3,)),
            sem((last, hp, sh)),
            sem((last, hp, sh)),
            sem((last, sh, PIECES)),
            sem((last, sh, PIECES)),
            sem((last, sh, PIECES)),
            sem((STEPS, 2, PIECES, sh)),
            sem((STEPS, PIECES, sh)),
            sem((STEPS, STEPS)),
            sem((STEPS, STEPS, hp)),
            sem((STEPS, STEPS)),
            sem((last, n_hist)),
            sem((last, hp)),
            sem((n_cut, hp)),
            sem((n_cut, hp)),
            sem((n_cut, nz)),
            sem((n_cut, nz)),
            sem((n_cut, nz)),
        ],
        compiler_params=pltpu.CompilerParams(
            collective_id=0, has_side_effects=True, vmem_limit_bytes=56 * 2**20
        ),
    )(history, self_energy, green_row, propagator)


def solution(mesh):
    in_specs = (
        P(None, "hist", "tgt", None, None),
        P(None, "hist", None, None),
        P(None, "tgt", None, None),
        P(),
    )
    out_specs = P(None, None, "tgt", "hist", None)
    return jax.shard_map(
        per_device, mesh=mesh, in_specs=in_specs, out_specs=out_specs, check_vma=False
    )
```

time: 117 us -> 120 us (1.026)
  Pallas kernels: 115 us -> 118 us
    pallas_call x1, Pallas kernels: 115 us -> 118 us  [per_device(): pl.pallas_call(functools.partial(kernel, n_tgt, n_hist, norm), out_shape=...]
where the time goes in v5:
time: 120 us
  Pallas kernels  118 us (98%)
  local copies, waits for them, and re-layouts  1.87 us (2%)
    pallas_call x1, Pallas kernels, per_device(): pl.pallas_call(functools.partial(kernel, n_tgt, n_hist, norm), out_shape=...  118 us

profile of v5, /device:TPU:0, one launch (start us, length us, event | category | flops | bytes accessed | tf_op | source)
XLA Modules:
  0.0 120.0 jit_solution(1538263392066918541)
XLA Ops:
  0.0 118.1 %shard_map.46 = f32[4,2,8,16,128]{4,3,2,1,0:T(8,128)} custom-call(f32[2,4,8,128,128]{4,3,2,1,0:T(8,128)} %h_hbm.1, f32[2,4,128,128]{3,2,1,0:T(8,128)} %s_hbm.1, f32[2,8,128,128]{3,2,1,0:T(8,128)} %r_hbm.1, f32[2,128,128]{2,1,0:T(8,128)} %p_hbm.1), custom_call_target="tpu_custom_call" | custom-call | tf_op jit(solution)/shard_map/pallas_call | solution.py:515
  118.1 1.9 %copy.6 = f32[4,2,8,16,128]{4,3,2,1,0:T(8,128)} copy(f32[4,2,8,16,128]{4,3,2,1,0:T(8,128)} %shard_map.46) | data formatting | bytes 1048576

commit v6 on v4

--- a/solution.py
+++ b/solution.py
@@ -47,6 +47,7 @@
     g, h = lax.axis_index("tgt"), lax.axis_index("hist")
     z, c = h // hp, h % hp
     root = z == g
+    middle = (z != g) & (z > 0) & (z < nz - 1)
     pos = snake(g)
     rel = (pos - snake(z) + n_tgt) % n_tgt
     ahead, behind = snake((pos + 1) % n_tgt), snake((pos + n_tgt - 1) % n_tgt)
@@ -69,8 +70,7 @@
     p_copy = pltpu.make_async_copy(p_hbm, pin, in_sem.at[1])
     r_copy = pltpu.make_async_copy(r_hbm, rin, in_sem.at[2])
     s_copy.start()
-    for d in [*range(1, hp), 0]:
-        loop(sh, lambda t, d=d: h_copy((c + d) % hp * sh + t).start())
+    loop(tt_all, lambda i: h_copy((c + i % hp + 1) % hp * sh + i // hp).start())
     p_copy.start()
     r_copy.start()
 
@@ -243,7 +243,6 @@
         loop(tt_all // 2, one)
         for s in range(half, sh):
             receive_s(step, s)
-        for s in range(half, sh):
             store_s3(step, s)
 
     def flush(waits):
@@ -305,6 +304,17 @@
                 for p in range(PIECES):
                     chain_copy(step, tt, p, False).start()
 
+        def relay(tt, step=step):
+            for up, here in ((True, z < g), (False, z > g)):
+
+                @pl.when(here)
+                def _():
+                    for p in range(PIECES):
+                        at = piece(p)
+                        chain_copy(step, tt, p, up).wait_recv()
+                        own[step, tt, :, at] += (upb if up else dnb)[step, tt, :, at]
+                        chain_copy(step, tt, p, up).start()
+
         def products(tt, step=step):
             terms = [term((c + d) % hp * sh + tt, step) for d in [*range(1, hp), 0]]
             for d in range(1, hp):
@@ -312,9 +322,11 @@
                 ex_copy(step, d, tt).start()
             own[step, tt, 0], own[step, tt, 1] = terms[hp - 1]
             pl.when(tt > 0)(lambda: first_link(tt - 1))
+            pl.when(middle & (tt > 1))(lambda: relay(tt - 2))
 
         loop(sh, products)
         first_link(sh - 1)
+        pl.when(middle)(lambda: loop(2, lambda i: relay(sh - 2 + i)))
         for d in range(1, hp):
             sends.append((None, lambda d=d, step=step: loop(sh, lambda tt: ex_copy(step, d, tt).wait_send())))
         if step == 0:
@@ -332,41 +344,28 @@
             for p in range(PIECES):
                 at = piece(p)
 
-                @pl.when((z > 0) & (z <= g))
+                @pl.when(z > 0)
                 def _():
                     chain_copy(step, tt, p, True).wait_recv()
                     own[step, tt, :, at] += upb[step, tt, :, at]
 
-                @pl.when((z < nz - 1) & (z >= g))
+                @pl.when(z < nz - 1)
                 def _():
                     chain_copy(step, tt, p, False).wait_recv()
                     own[step, tt, :, at] += dnb[step, tt, :, at]
 
-                @pl.when((z < g) & (z > 0))
-                def _():
-                    chain_copy(step, tt, p, True).start()
-
-                @pl.when((z > g) & (z < nz - 1))
-                def _():
-                    chain_copy(step, tt, p, False).start()
-
-                @pl.when(root)
-                def _():
-                    real = own[step, tt, 0, at] + base[tt, 0, at]
-                    imag = own[step, tt, 1, at] + base[tt, 1, at]
-                    modulus = real * real + imag * imag
-                    factor = -COUPLING * modulus / (1.0 + modulus)
-                    sbuf[step + 1, 0, tt, at] = factor * real
-                    sbuf[step + 1, 1, tt, at] = factor * imag
-                    ring_give(step + 1, tt, p)
-                    rows[step, 0, tt, at] = real
-                    rows[step, 1, tt, at] = imag
-
-            @pl.when(root)
-            def _():
-                store_x3(step + 1, tt, rows[step, 0, tt], rows[step, 1, tt])
-
-        loop(sh, link)
+                real = own[step, tt, 0, at] + base[tt, 0, at]
+                imag = own[step, tt, 1, at] + base[tt, 1, at]
+                modulus = real * real + imag * imag
+                factor = -COUPLING * modulus / (1.0 + modulus)
+                sbuf[step + 1, 0, tt, at] = factor * real
+                sbuf[step + 1, 1, tt, at] = factor * imag
+                ring_give(step + 1, tt, p)
+                rows[step, 0, tt, at] = real
+                rows[step, 1, tt, at] = imag
+            store_x3(step + 1, tt, rows[step, 0, tt], rows[step, 1, tt])
+
+        pl.when(root)(lambda: loop(sh, link))
         for up, gives in ((True, z < g), (False, z > g)):
             for p in range(PIECES):
                 sends.append(
@@ -456,9 +455,10 @@
             sends.append((None, lambda u=u, d=d: fin_ex_copy(u, d).wait_send()))
         if u > 0:
             of_pair(u - 1)
+        if u > 1:
+            far(u - 2, far_next)
     of_pair(n_cut - 1)
-
-    for u in range(n_cut):
+    for u in range(max(0, n_cut - 2), n_cut):
         far(u, far_next)
     for step in range(last):
         for sender in range(hp):

time: 117 us -> 118 us (level)
  no operation moved by 1% of the time
where the time goes in v6:
time: 118 us; the launch traced here: 117 us
  Pallas kernels  115 us (97%)
  local copies, waits for them, and re-layouts  1.87 us (2%)
    pallas_call x1, Pallas kernels, per_device(): pl.pallas_call(functools.partial(kernel, n_tgt, n_hist, norm), out_shape=...  115 us

profile of v6, /device:TPU:0, one launch (start us, length us, event | category | flops | bytes accessed | tf_op | source)
XLA Modules:
  0.0 116.9 jit_solution(9122370174340789739)
XLA Ops:
  0.0 115.0 %shard_map.46 = f32[4,2,8,16,128]{4,3,2,1,0:T(8,128)} custom-call(f32[2,4,8,128,128]{4,3,2,1,0:T(8,128)} %h_hbm.1, f32[2,4,128,128]{3,2,1,0:T(8,128)} %s_hbm.1, f32[2,8,128,128]{3,2,1,0:T(8,128)} %r_hbm.1, f32[2,128,128]{2,1,0:T(8,128)} %p_hbm.1), custom_call_target="tpu_custom_call" | custom-call | tf_op jit(solution)/shard_map/pallas_call | solution.py:500
  115.0 1.9 %copy.6 = f32[4,2,8,16,128]{4,3,2,1,0:T(8,128)} copy(f32[4,2,8,16,128]{4,3,2,1,0:T(8,128)} %shard_map.46) | data formatting | bytes 1048576
